TPU v7x, 128 devices: a whole 4x4x4 slice. The times are simulated.
128 devices in a mesh: lat: 8 (over z_lo, x), lon: 16 (over y, z_hi, core).
Axes of the slice: x: 4, y: 4, z: 4 (z_hi: 2, z_lo: 2; z = z_hi * 2 + z_lo), core: 2. Of those that a mesh axis runs over, the one named last changes fastest.
Arguments:
- background: float32 [2, 25, 512, 2048], P(None, None, 'lat', 'lon'), may hold values from -6 to 6
- error_scale: float32 [2, 25, 512, 2048], P(None, None, 'lat', 'lon'), may hold values from 0.5 to 2
- east_rate: float32 [512, 2048], P('lat', 'lon'), may hold values from 0.05 to 0.24
- north_rate: float32 [512, 2048], P('lat', 'lon'), may hold values from 0.05 to 0.24
- sea_mask: int32 [512, 2048], P('lat', 'lon'), may hold values 0 or 1
- partner: int32 [2048], replicated, may hold values from 0 to 2047, as said below
- obs_weight: float32 [128, 128, 50, 128], P(('lat', 'lon')), may hold values from -0.875 to 0.875
- obs_value: float32 [128, 128, 128], P(('lat', 'lon')), may hold values from -8 to 8
- obs_error: float32 [128, 128, 128], P(('lat', 'lon')), may hold values from 0.5 to 2
- obs_column: int32 [128, 128, 128], P(('lat', 'lon')), may hold values from 0 to 8191
- obs_count: int32 [128, 128], P(('lat', 'lon')), may hold values from 0 to 128, as said below
Outputs:
- increment: float32 [2, 25, 512, 2048], P(None, None, 'lat', 'lon')
- cost_share: float32 [], replicated
Inputs may be any that keep to these rules, and one draw needn't show every extreme that they name: `obs_count`: every source device fills all 128 slots to at least one owner, and one owner gets all 128 slots from every source. partner[g] = (s - g) modulo 2048 for one s, so partner[partner[g]] = g.
All inputs are finite; a program needn't handle non-finite values. No bound on the sum of `sea_mask` on one device may be relied on, other than what follows from the above.
Results may differ from a plain program's by a relative error of at most 0.0003.
Values sent between devices are 32-bit elements; how exact they have to be, the bound alone decides.
No kernel may reach another device: no remote copies, remote signals or barrier semaphores. Data moves between devices by JAX's collectives and lax.ppermute only.
A program may use at most 128 MiB of HBM per device.

v0:
```python
import jax
import jax.numpy as jnp
from jax import lax
from jax.sharding import PartitionSpec as P

STEPS = 4


huber_edge = 1.5


def with_halo(cells, sides, width):
    for axis, dim in sides:
        count = lax.axis_size(axis)
        head = lax.slice_in_dim(cells, 0, width, axis=dim)
        tail = lax.slice_in_dim(cells, cells.shape[dim] - width, cells.shape[dim], axis=dim)
        cells = jnp.concatenate(
            [
                lax.ppermute(tail, axis, [(i, (i + 1) % count) for i in range(count)]),
                cells,
                lax.ppermute(head, axis, [((i + 1) % count, i) for i in range(count)]),
            ],
            axis=dim,
        )
    return cells


def relax(ext_field, ext_coef):
    center = ext_field[:, 1:-1, 1:-1]
    sea_here = ext_coef[2, 1:-1, 1:-1]
    east_here = ext_coef[0, 1:-1, 1:-1]
    north_here = ext_coef[1, 1:-1, 1:-1]
    along_term = ext_coef[2, 1:-1, 2:] * (ext_field[:, 1:-1, 2:] - center) + ext_coef[
        2, 1:-1, :-2
    ] * (ext_field[:, 1:-1, :-2] - center)
    across = ext_coef[2, 2:, 1:-1] * (ext_field[:, 2:, 1:-1] - center) + ext_coef[2, :-2, 1:-1] * (
        ext_field[:, :-2, 1:-1] - center
    )
    return center + sea_here * (east_here * along_term + north_here * across)


def extend(field_in, rim_depth, partner):
    pieces = with_halo(field_in, (("lat", 1), ("lon", 2)), rim_depth)
    band_index = lax.axis_index("lat")
    strip_index = lax.axis_index("lon")
    row_width = field_in.shape[2]
    lon_total = row_width * lax.axis_size("lon")
    top_rows = lax.all_gather(
        field_in[:, field_in.shape[1] - rim_depth :, :], "lon", axis=2, tiled=True
    )
    mirrored = top_rows[:, ::-1, :]
    columns = (
        strip_index * row_width - rim_depth + jnp.arange(row_width + 2 * rim_depth, dtype=jnp.int32)
    ) % lon_total
    ghost_rows = jnp.take(mirrored, partner[columns], axis=2)
    height = pieces.shape[1]
    north_rows = jnp.where(
        band_index == lax.axis_size("lat") - 1, ghost_rows, pieces[:, height - rim_depth :, :]
    )
    south_rows = jnp.where(band_index == 0, jnp.zeros_like(ghost_rows), pieces[:, :rim_depth, :])
    return jnp.concatenate(
        [south_rows, pieces[:, rim_depth : height - rim_depth, :], north_rows], axis=1
    )


def shards(
    background,
    error_scale,
    east_rate,
    north_rate,
    sea_mask,
    partner,
    obs_weight,
    obs_value,
    obs_error,
    obs_column,
    obs_count,
):
    levels = background.shape[0] * background.shape[1]
    lat_cells = background.shape[2]
    lon_cells = background.shape[3]
    capacity = obs_weight.shape[3]
    owners = obs_weight.shape[1]
    slot_index = lax.broadcasted_iota(jnp.int32, (owners, capacity), 1)
    valid_slot = slot_index < obs_count[0][:, None]
    inverse = jnp.where(valid_slot, 1.0 / obs_error[0], 0.0)
    packed = jnp.concatenate(
        [
            obs_weight[0],
            obs_value[0][:, None, :],
            inverse[:, None, :],
            obs_column[0].astype(jnp.float32)[:, None, :],
        ],
        axis=1,
    )
    received = lax.all_to_all(packed, ("lat", "lon"), split_axis=0, concat_axis=0, tiled=True)
    weights = jnp.swapaxes(received[:, :levels, :], 0, 1)
    values_in = received[:, levels, :]
    inverse_in = received[:, levels + 1, :]
    cells_in = received[:, levels + 2, :].astype(jnp.int32)
    flat_bg = background.reshape(levels, lat_cells * lon_cells)
    sampled = flat_bg[:, cells_in]
    equiv = jnp.sum(weights * sampled, axis=0)
    scaled = (values_in - equiv) * inverse_in
    magnitude = jnp.abs(scaled)
    huber_terms = jnp.where(
        magnitude <= huber_edge,
        0.5 * scaled * scaled,
        huber_edge * magnitude - 0.5 * huber_edge * huber_edge,
    )
    response = huber_edge / jnp.maximum(magnitude, huber_edge) * scaled * inverse_in
    forcing = (
        jnp.zeros((levels, lat_cells * lon_cells), jnp.float32)
        .at[:, cells_in.reshape(-1)]
        .add((weights * response[None]).reshape(levels, -1))
    )
    sea_float = sea_mask.astype(jnp.float32)
    spread = error_scale.reshape(levels, lat_cells, lon_cells)
    state = sea_float[None] * spread * forcing.reshape(levels, lat_cells, lon_cells)
    coefficients = jnp.stack([east_rate, north_rate, sea_float])
    coef_ext = extend(coefficients, 1, partner)
    for sweep_index in range(STEPS):
        state = relax(extend(state, 1, partner), coef_ext)
    increment = (spread * state).reshape(background.shape)
    cost_share = lax.psum(jnp.sum(huber_terms), ("lat", "lon")) / (owners * owners * capacity)
    return (increment, cost_share)


def solution(mesh):
    in_specs = (
        P(None, None, "lat", "lon"),
        P(None, None, "lat", "lon"),
        P("lat", "lon"),
        P("lat", "lon"),
        P("lat", "lon"),
        P(),
        P(("lat", "lon"), None, None, None),
        P(("lat", "lon"), None, None),
        P(("lat", "lon"), None, None),
        P(("lat", "lon"), None, None),
        P(("lat", "lon"), None),
    )
    out_specs = (P(None, None, "lat", "lon"), P())
    return jax.shard_map(shards, mesh=mesh, in_specs=in_specs, out_specs=out_specs, check_vma=False)
```

profile of v0, /device:TPU:6, one launch (start us, length us, event | category | flops | bytes accessed | tf_op | source)
XLA Modules:
  0.0 587.7 jit_solution(16315026287155382560)
XLA Ops:
  8.7 10.9 %all-to-all-start = ((f32[128,53,128]{2,1,0:T(8,128)}), f32[128,53,128]{2,1,0:T(8,128)}, u32[]{:S(2)}, u32[]{:S(2)}) async-start(f32[128,53,128]{2,1,0:T(8,128)} %pad_maximum_fusion.45), calls=%async_computation | async-start | bytes 7340032 | tf_op jit(solution)/shard_map/all_to_all | solution.py:96
  29.1 59.1 %all_gather.15 = f32[3,1,2048]{0,2,1:T(8,128)} all-gather(f32[3,1,128]{0,2,1:T(8,128)S(1)} %get-tuple-element.35), channel_id=1, replica_groups=mesh['lat'=8,'lon'=16] {'lon'}, dimensions={2}, use_global_device_ids=true | all-gather | bytes 26112 | tf_op jit(solution)/shard_map/all_gather | solution.py:48
  90.3 5.4 collective-permute-start.2
  112.1 9.6 %fusion.64 = (f32[64,128]{1,0:T(8,128)S(1)}, f32[64,128]{1,0:T(8,128)S(1)}) fusion(f32[3,66,1]{0,2,1:T(1,128)} %collective-permute-done.2, f32[3,1,128]{0,2,1:T(8,128)S(1)} %copy-done.16, f32[3,64,128]{0,2,1:T(8,128)S(1)} %copy-done.8, f32[3,1,128]{0,2,1:T(8,128)S(1)} %copy-done.18, f32[3,66,1]{0,2,1:T(1,128)} %collective-permute-done.6), kind=kLoop, calls=%fused_computation.115 | loop fusion | flops 49152 | bytes 168496 | tf_op jit(solution)/shard_map/slice | solution.py:33
  123.6 56.7 %gather_fusion = f32[16384,50]{1,0:T(8,128)} fusion(f32[50,8192]{0,1:T(8,128)} %copy.155, s32[16384]{0:T(1024)S(1)} %fusion.72), kind=kCustom, calls=%fused_computation.4 | custom fusion | bytes 6619136 | tf_op jit(solution)/shard_map/gather | solution.py:102
  180.2 6.8 %copy.156 = f32[128,128,50]{1,2,0:T(8,128)} copy(f32[128,128,50]{2,1,0:T(8,128)} %bitcast.85) | data formatting | bytes 6553600 | tf_op jit(solution)/shard_map/gather | solution.py:102
  198.8 7.1 %copy.158 = f32[16384,50]{1,0:T(8,128)} copy(f32[16384,50]{0,1:T(8,128)} %bitcast.88) | data formatting | bytes 6553600 | tf_op jit(solution)/shard_map/reshape | solution.py:115
  207.1 89.8 %scatter_custom_fusion = f32[50,8192]{0,1:T(8,128)} fusion(s32[16384]{0:T(1024)S(1)} %bitcast.107, f32[16384,50]{1,0:T(8,128)} %copy.158, f32[]{:T(128)} %constant.45.clone.1), kind=kCustom, calls=%fused_computation.125 | custom fusion | flops 819200 | bytes 1638912 | tf_op jit(solution)/shard_map/scatter-add | solution.py:115
  305.4 4.4 fusion.56
  310.0 5.3 collective-permute-start.5
  315.4 23.3 %all_gather.16 = f32[50,1,2048]{0,2,1:T(8,128)S(1)} all-gather(f32[50,1,128]{0,2,1:T(8,128)S(1)} %get-tuple-element.37), channel_id=1, replica_groups=mesh['lat'=8,'lon'=16] {'lon'}, dimensions={2}, use_global_device_ids=true | all-gather | bytes 435200 | tf_op jit(solution)/shard_map/all_gather | solution.py:48
  345.1 9.8 %fusion.52 = f32[50,64,128]{0,2,1:T(8,128)S(1)} fusion(f32[50,64,128]{0,2,1:T(8,128)S(1)} %copy-done.3, f32[50,64,130]{0,2,1:T(8,128)S(1)} %slice.339, f32[50,1,130]{0,2,1:T(8,128)S(1)} %get-tuple-element.18, f32[50,1,130]{0,2,1:T(8,128)S(1)} %get-tuple-element.17, f32[50,66,1]{0,2,1:T(1,128)S(1)} %collective-permute-done.7, ...), kind=kLoop, calls=%fused_computation.90 | loop fusion | flops 9420800 | bytes 5299776 | tf_op jit(solution)/shard_map/add | solution.py:39
  355.1 4.5 collective-permute-start.8
  361.7 5.3 collective-permute-start.10
  367.0 22.7 %all_gather.17 = f32[50,1,2048]{0,2,1:T(8,128)S(1)} all-gather(f32[50,1,128]{0,2,1:T(8,128)S(1)} %get-tuple-element.33), channel_id=1, replica_groups=mesh['lat'=8,'lon'=16] {'lon'}, dimensions={2}, use_global_device_ids=true | all-gather | bytes 435200 | tf_op jit(solution)/shard_map/all_gather | solution.py:48
  395.5 9.9 %fusion.37 = f32[50,64,128]{0,2,1:T(8,128)S(1)} fusion(f32[50,64,128]{0,2,1:T(8,128)S(1)} %copy-done.5, f32[50,64,130]{0,2,1:T(8,128)S(1)} %slice.342, f32[50,1,130]{0,2,1:T(8,128)S(1)} %get-tuple-element.14, f32[50,1,130]{0,2,1:T(8,128)S(1)} %get-tuple-element.13, f32[50,66,1]{0,2,1:T(1,128)S(1)} %collective-permute-done.11, ...), kind=kLoop, calls=%fused_computation.67 | loop fusion | flops 9420800 | bytes 5299776 | tf_op jit(solution)/shard_map/add | solution.py:39
  405.5 5.9 %collective-permute-start.12 = (f32[50,1,128]{0,2,1:T(8,128)S(1)}, f32[50,1,128]{0,2,1:T(8,128)S(1)}, u32[]{:S(2)}, u32[]{:S(2)}) collective-permute-start(f32[50,1,128]{0,2,1:T(8,128)S(1)} %get-tuple-element.31), channel_id=1, source_target_pairs={{0,16},{16,32},{32,48},{48,64},{64,80},{80,96},{96,112},{112,0},{1... | collective-permute-start | bytes 76808 | tf_op jit(solution)/shard_map/ppermute | solution.py:19
  414.1 5.3 collective-permute-start.14
  419.4 24.3 %all_gather.18 = f32[50,1,2048]{0,2,1:T(8,128)S(1)} all-gather(f32[50,1,128]{0,2,1:T(8,128)S(1)} %get-tuple-element.31), channel_id=1, replica_groups=mesh['lat'=8,'lon'=16] {'lon'}, dimensions={2}, use_global_device_ids=true | all-gather | bytes 435200 | tf_op jit(solution)/shard_map/all_gather | solution.py:48
  449.4 9.9 %fusion.22 = f32[50,64,128]{0,2,1:T(8,128)S(1)} fusion(f32[50,64,128]{0,2,1:T(8,128)S(1)} %copy-done.7, f32[50,64,130]{0,2,1:T(8,128)S(1)} %slice.345, f32[50,1,130]{0,2,1:T(8,128)S(1)} %get-tuple-element.12, f32[50,1,130]{0,2,1:T(8,128)S(1)} %get-tuple-element.11, f32[50,66,1]{0,2,1:T(1,128)S(1)} %collective-permute-done.15, ...), kind=kLoop, calls=%fused_computation.44 | loop fusion | flops 9420800 | bytes 5299776 | tf_op jit(solution)/shard_map/add | solution.py:39
  465.5 64.6 %psum.7 = f32[]{:T(128)} all-reduce(f32[]{:T(128)} %get-tuple-element.42), channel_id=1, replica_groups=mesh['lat'=8,'lon'=16] {'lat','lon'}, use_global_device_ids=true, to_apply=%region_3.5 | all-reduce | flops 1 | bytes 8 | tf_op jit(solution)/shard_map/psum | solution.py:125
  531.9 5.3 collective-permute-start.18
  537.3 23.3 %all_gather.19 = f32[50,1,2048]{0,2,1:T(8,128)S(1)} all-gather(f32[50,1,128]{0,2,1:T(8,128)S(1)} %get-tuple-element.29), channel_id=1, replica_groups=mesh['lat'=8,'lon'=16] {'lon'}, dimensions={2}, use_global_device_ids=true | all-gather | bytes 435200 | tf_op jit(solution)/shard_map/all_gather | solution.py:48
  568.4 13.9 %fusion.7 = f32[50,64,128]{0,2,1:T(8,128)} fusion(f32[50,64,128]{0,2,1:T(8,128)S(1)} %copy-done.11, f32[50,64,128]{0,2,1:T(8,128)S(1)} %copy-done.10, f32[50,64,130]{0,2,1:T(8,128)S(1)} %slice.348, f32[50,1,130]{0,2,1:T(8,128)S(1)} %get-tuple-element.10, f32[50,1,130]{0,2,1:T(8,128)S(1)} %get-tuple-element.9, f32[50,66,1]{0,2,1:T(1,128)S(1)} %collective-permute-done.19, ...), kind=kLoop, calls=%fused_computation.21 | loop fusion | flops 9830400 | bytes 6938176 | tf_op jit(solution)/shard_map/mul | solution.py:124
  (146 shorter events, 101.1 us)
Async XLA Ops:
  0.6 26.9 %copy-start = (s32[2048]{0:T(1024)S(1)}, s32[2048]{0:T(1024)}, u32[]{:S(2)}) copy-start(s32[2048]{0:T(1024)} %param.18) | copy-start | bytes 24580
  8.7 113.0 %all-to-all-start = ((f32[128,53,128]{2,1,0:T(8,128)}), f32[128,53,128]{2,1,0:T(8,128)}, u32[]{:S(2)}, u32[]{:S(2)}) async-start(f32[128,53,128]{2,1,0:T(8,128)} %pad_maximum_fusion.45), calls=%async_computation | async-start | bytes 7340032 | tf_op jit(solution)/shard_map/all_to_all | solution.py:96
  22.3 73.4 %copy-start.13 = (f32[2,25,64,128]{3,2,1,0:T(8,128)S(1)}, f32[2,25,64,128]{3,2,1,0:T(8,128)}, u32[]{:S(2)}) copy-start(f32[2,25,64,128]{3,2,1,0:T(8,128)} %param.13) | copy-start | bytes 4915204
  23.3 64.9 %collective-permute-start.1 = (f32[3,1,128]{0,2,1:T(8,128)S(1)}, f32[3,1,128]{0,2,1:T(8,128)S(1)}, u32[]{:S(2)}, u32[]{:S(2)}) collective-permute-start(f32[3,1,128]{0,2,1:T(8,128)S(1)} %get-tuple-element.36), channel_id=1, source_target_pairs={{16,0},{32,16},{48,32},{64,48},{80,64},{96,80},{112,96},{0,112},{1... | collective-permute-start | bytes 4616 | tf_op jit(solution)/shard_map/ppermute | solution.py:21
  24.2 63.9 %collective-permute-start = (f32[3,1,128]{0,2,1:T(8,128)S(1)}, f32[3,1,128]{0,2,1:T(8,128)S(1)}, u32[]{:S(2)}, u32[]{:S(2)}) collective-permute-start(f32[3,1,128]{0,2,1:T(8,128)S(1)} %get-tuple-element.35), channel_id=1, source_target_pairs={{0,16},{16,32},{32,48},{48,64},{64,80},{80,96},{96,112},{112,0},{1... | collective-permute-start | bytes 4616 | tf_op jit(solution)/shard_map/ppermute | solution.py:19
  90.0 14.7 %collective-permute-start.6 = (f32[3,66,1]{0,2,1:T(1,128)}, f32[3,66,1]{0,2,1:T(1,128)}, u32[]{:S(2)}, u32[]{:S(2)}) collective-permute-start(f32[3,66,1]{0,2,1:T(1,128)} %get-tuple-element.25), channel_id=1, source_target_pairs={{0,1},{1,2},{2,3},{3,4},{4,5},{5,6},{6,7},{7,8},{8,9},{9,10},{10,1... | collective-permute-start | bytes 2384 | tf_op jit(solution)/shard_map/ppermute | solution.py:19
  90.3 14.3 %collective-permute-start.2 = (f32[3,66,1]{0,2,1:T(1,128)}, f32[3,66,1]{0,2,1:T(1,128)}, u32[]{:S(2)}, u32[]{:S(2)}) collective-permute-start(f32[3,66,1]{0,2,1:T(1,128)} %get-tuple-element.26), channel_id=1, source_target_pairs={{1,0},{2,1},{3,2},{4,3},{5,4},{6,5},{7,6},{8,7},{9,8},{10,9},{11,1... | collective-permute-start | bytes 2384 | tf_op jit(solution)/shard_map/ppermute | solution.py:21
  301.2 8.6 %collective-permute-start.4 = (f32[50,1,128]{0,2,1:T(8,128)S(1)}, f32[50,1,128]{0,2,1:T(8,128)S(1)}, u32[]{:S(2)}, u32[]{:S(2)}) collective-permute-start(f32[50,1,128]{0,2,1:T(8,128)S(1)} %get-tuple-element.38), channel_id=1, source_target_pairs={{16,0},{32,16},{48,32},{64,48},{80,64},{96,80},{112,96},{0,112},{1... | collective-permute-start | bytes 76808 | tf_op jit(solution)/shard_map/ppermute | solution.py:21
  301.3 8.6 %collective-permute-start.3 = (f32[50,1,128]{0,2,1:T(8,128)S(1)}, f32[50,1,128]{0,2,1:T(8,128)S(1)}, u32[]{:S(2)}, u32[]{:S(2)}) collective-permute-start(f32[50,1,128]{0,2,1:T(8,128)S(1)} %get-tuple-element.37), channel_id=1, source_target_pairs={{0,16},{16,32},{32,48},{48,64},{64,80},{80,96},{96,112},{112,0},{1... | collective-permute-start | bytes 76808 | tf_op jit(solution)/shard_map/ppermute | solution.py:19
  309.9 29.4 %collective-permute-start.7 = (f32[50,66,1]{0,2,1:T(1,128)S(1)}, f32[50,66,1]{0,2,1:T(1,128)S(1)}, u32[]{:S(2)}, u32[]{:S(2)}) collective-permute-start(f32[50,66,1]{0,2,1:T(1,128)S(1)} %get-tuple-element.27), channel_id=1, source_target_pairs={{0,1},{1,2},{2,3},{3,4},{4,5},{5,6},{6,7},{7,8},{8,9},{9,10},{10,1... | collective-permute-start | bytes 39608 | tf_op jit(solution)/shard_map/ppermute | solution.py:19
  310.0 29.3 %collective-permute-start.5 = (f32[50,66,1]{0,2,1:T(1,128)S(1)}, f32[50,66,1]{0,2,1:T(1,128)S(1)}, u32[]{:S(2)}, u32[]{:S(2)}) collective-permute-start(f32[50,66,1]{0,2,1:T(1,128)S(1)} %get-tuple-element.28), channel_id=1, source_target_pairs={{1,0},{2,1},{3,2},{4,3},{5,4},{6,5},{7,6},{8,7},{9,8},{10,9},{11,1... | collective-permute-start | bytes 39608 | tf_op jit(solution)/shard_map/ppermute | solution.py:21
  355.0 6.5 %collective-permute-start.9 = (f32[50,1,128]{0,2,1:T(8,128)S(1)}, f32[50,1,128]{0,2,1:T(8,128)S(1)}, u32[]{:S(2)}, u32[]{:S(2)}) collective-permute-start(f32[50,1,128]{0,2,1:T(8,128)S(1)} %get-tuple-element.34), channel_id=1, source_target_pairs={{16,0},{32,16},{48,32},{64,48},{80,64},{96,80},{112,96},{0,112},{1... | collective-permute-start | bytes 76808 | tf_op jit(solution)/shard_map/ppermute | solution.py:21
  355.1 6.4 %collective-permute-start.8 = (f32[50,1,128]{0,2,1:T(8,128)S(1)}, f32[50,1,128]{0,2,1:T(8,128)S(1)}, u32[]{:S(2)}, u32[]{:S(2)}) collective-permute-start(f32[50,1,128]{0,2,1:T(8,128)S(1)} %get-tuple-element.33), channel_id=1, source_target_pairs={{0,16},{16,32},{32,48},{48,64},{64,80},{80,96},{96,112},{112,0},{1... | collective-permute-start | bytes 76808 | tf_op jit(solution)/shard_map/ppermute | solution.py:19
  361.6 28.8 %collective-permute-start.11 = (f32[50,66,1]{0,2,1:T(1,128)S(1)}, f32[50,66,1]{0,2,1:T(1,128)S(1)}, u32[]{:S(2)}, u32[]{:S(2)}) collective-permute-start(f32[50,66,1]{0,2,1:T(1,128)S(1)} %get-tuple-element.23), channel_id=1, source_target_pairs={{0,1},{1,2},{2,3},{3,4},{4,5},{5,6},{6,7},{7,8},{8,9},{9,10},{10,1... | collective-permute-start | bytes 39608 | tf_op jit(solution)/shard_map/ppermute | solution.py:19
  361.7 28.7 %collective-permute-start.10 = (f32[50,66,1]{0,2,1:T(1,128)S(1)}, f32[50,66,1]{0,2,1:T(1,128)S(1)}, u32[]{:S(2)}, u32[]{:S(2)}) collective-permute-start(f32[50,66,1]{0,2,1:T(1,128)S(1)} %get-tuple-element.24), channel_id=1, source_target_pairs={{1,0},{2,1},{3,2},{4,3},{5,4},{6,5},{7,6},{8,7},{9,8},{10,9},{11,1... | collective-permute-start | bytes 39608 | tf_op jit(solution)/shard_map/ppermute | solution.py:21
  405.4 8.5 %collective-permute-start.13 = (f32[50,1,128]{0,2,1:T(8,128)S(1)}, f32[50,1,128]{0,2,1:T(8,128)S(1)}, u32[]{:S(2)}, u32[]{:S(2)}) collective-permute-start(f32[50,1,128]{0,2,1:T(8,128)S(1)} %get-tuple-element.32), channel_id=1, source_target_pairs={{16,0},{32,16},{48,32},{64,48},{80,64},{96,80},{112,96},{0,112},{1... | collective-permute-start | bytes 76808 | tf_op jit(solution)/shard_map/ppermute | solution.py:21
  405.5 8.5 %collective-permute-start.12 = (f32[50,1,128]{0,2,1:T(8,128)S(1)}, f32[50,1,128]{0,2,1:T(8,128)S(1)}, u32[]{:S(2)}, u32[]{:S(2)}) collective-permute-start(f32[50,1,128]{0,2,1:T(8,128)S(1)} %get-tuple-element.31), channel_id=1, source_target_pairs={{0,16},{16,32},{32,48},{48,64},{64,80},{80,96},{96,112},{112,0},{1... | collective-permute-start | bytes 76808 | tf_op jit(solution)/shard_map/ppermute | solution.py:19
  414.0 30.3 %collective-permute-start.15 = (f32[50,66,1]{0,2,1:T(1,128)S(1)}, f32[50,66,1]{0,2,1:T(1,128)S(1)}, u32[]{:S(2)}, u32[]{:S(2)}) collective-permute-start(f32[50,66,1]{0,2,1:T(1,128)S(1)} %get-tuple-element.21), channel_id=1, source_target_pairs={{0,1},{1,2},{2,3},{3,4},{4,5},{5,6},{6,7},{7,8},{8,9},{9,10},{10,1... | collective-permute-start | bytes 39608 | tf_op jit(solution)/shard_map/ppermute | solution.py:19
  414.1 30.3 %collective-permute-start.14 = (f32[50,66,1]{0,2,1:T(1,128)S(1)}, f32[50,66,1]{0,2,1:T(1,128)S(1)}, u32[]{:S(2)}, u32[]{:S(2)}) collective-permute-start(f32[50,66,1]{0,2,1:T(1,128)S(1)} %get-tuple-element.22), channel_id=1, source_target_pairs={{1,0},{2,1},{3,2},{4,3},{5,4},{6,5},{7,6},{8,7},{9,8},{10,9},{11,1... | collective-permute-start | bytes 39608 | tf_op jit(solution)/shard_map/ppermute | solution.py:21
  461.3 69.4 %collective-permute-start.17 = (f32[50,1,128]{0,2,1:T(8,128)S(1)}, f32[50,1,128]{0,2,1:T(8,128)S(1)}, u32[]{:S(2)}, u32[]{:S(2)}) collective-permute-start(f32[50,1,128]{0,2,1:T(8,128)S(1)} %get-tuple-element.30), channel_id=1, source_target_pairs={{16,0},{32,16},{48,32},{64,48},{80,64},{96,80},{112,96},{0,112},{1... | collective-permute-start | bytes 76808 | tf_op jit(solution)/shard_map/ppermute | solution.py:21
  461.4 69.4 %collective-permute-start.16 = (f32[50,1,128]{0,2,1:T(8,128)S(1)}, f32[50,1,128]{0,2,1:T(8,128)S(1)}, u32[]{:S(2)}, u32[]{:S(2)}) collective-permute-start(f32[50,1,128]{0,2,1:T(8,128)S(1)} %get-tuple-element.29), channel_id=1, source_target_pairs={{0,16},{16,32},{32,48},{48,64},{64,80},{80,96},{96,112},{112,0},{1... | collective-permute-start | bytes 76808 | tf_op jit(solution)/shard_map/ppermute | solution.py:19
  531.9 29.4 %collective-permute-start.19 = (f32[50,66,1]{0,2,1:T(1,128)S(1)}, f32[50,66,1]{0,2,1:T(1,128)S(1)}, u32[]{:S(2)}, u32[]{:S(2)}) collective-permute-start(f32[50,66,1]{0,2,1:T(1,128)S(1)} %get-tuple-element.19), channel_id=1, source_target_pairs={{0,1},{1,2},{2,3},{3,4},{4,5},{5,6},{6,7},{7,8},{8,9},{9,10},{10,1... | collective-permute-start | bytes 39608 | tf_op jit(solution)/shard_map/ppermute | solution.py:19
  531.9 29.3 %collective-permute-start.18 = (f32[50,66,1]{0,2,1:T(1,128)S(1)}, f32[50,66,1]{0,2,1:T(1,128)S(1)}, u32[]{:S(2)}, u32[]{:S(2)}) collective-permute-start(f32[50,66,1]{0,2,1:T(1,128)S(1)} %get-tuple-element.20), channel_id=1, source_target_pairs={{1,0},{2,1},{3,2},{4,3},{5,4},{6,5},{7,6},{8,7},{9,8},{10,9},{11,1... | collective-permute-start | bytes 39608 | tf_op jit(solution)/shard_map/ppermute | solution.py:21
  568.4 18.0 %copy-start.1 = (s32[2048]{0:T(1024)S(1)}, s32[2048]{0:T(1024)}, u32[]{:S(2)}) copy-start(s32[2048]{0:T(1024)} %param.18) | copy-start | bytes 24580
  (23 other events, 125.3 us)
where the time goes:
time: 597 us; the launch traced here: 588 us
  blocking collectives  217 us (36%)
  other arithmetic  184 us (31%)
  local copies, waits for them, and re-layouts  117 us (20%)
  starting transfers between devices  61.5 us (10%)
    all_gather x5, blocking collectives, extend(): lax.all_gather(field_in[:, field_in.shape[1] - rim_depth:, :], 'lon', axi...  153 us
    scatter-add x1, other arithmetic, shards(): forcing = jnp.zeros((levels, lat_cells * lon_cells), jnp.float32).at[:, c...  89.8 us
    psum x1, blocking collectives, shards(): lax.psum(jnp.sum(huber_terms), ('lat', 'lon'))  64.6 us
    gather x2, local copies, waits for them, and re-layouts, shards(): sampled = flat_bg[:, cells_in]  63.4 us
    add x3, other arithmetic, relax(): return center + sea_here * (east_here * along_term + north_here * across)  29.6 us
    ppermute x10, starting transfers between devices, with_halo(): lax.ppermute(head, axis, [((i + 1) % count, i) for i in range(count)])  28 us
    unnamed x55, local copies, waits for them, and re-layouts  25.6 us
    ppermute x10, starting transfers between devices, with_halo(): lax.ppermute(tail, axis, [(i, (i + 1) % count) for i in range(count)])  22.6 us
  transfers between devices with their start and end apart: 21, of which 2 were waited for; matrix products, arithmetic and copies ran while one was open for 6% of the time, Pallas kernels for 0%

commit v1 on v0

v1 whole, which is shorter than its diff:
```python
import jax
import jax.numpy as jnp
from jax import lax
from jax.experimental import pallas as pl
from jax.experimental.pallas import tpu as pltpu
from jax.sharding import PartitionSpec as P

STEPS = 4
HALO = 4
HUBER_EDGE = 1.5
F32 = jnp.float32
BF16 = jnp.bfloat16
VMEM_LIMIT = 56 * 1024 * 1024


def split_background(bg_ref, out_ref):
    levels = bg_ref.shape[0]
    for h in range(4):
        for p in range(2):
            base = (2 * h + p) * levels * 8
            row = 32 * p + 8 * h

            def body(i, _):
                a = bg_ref[2 * i, row : row + 8, :]
                b = bg_ref[2 * i + 1, row : row + 8, :]
                x = jnp.concatenate([a, b], axis=0)
                hi = x.astype(BF16)
                lo = (x - hi.astype(F32)).astype(BF16)
                at = pl.ds(pl.multiple_of(base + i * 16, 16), 16)
                out_ref[at, 0:128] = hi
                out_ref[at, 128:256] = lo
                return 0

            lax.fori_loop(0, levels // 2, body, 0, unroll=5)


def observe(rec_ref, bgm_ref, sea_ref, es_ref, state_ref, cost_ref, tiles, force, whi, wlo, amat):
    step = pl.program_id(0)
    steps = pl.num_programs(0)
    levels = es_ref.shape[0]
    rows_in = 8 * levels

    @pl.when(step == 0)
    def _():
        force[...] = jnp.zeros_like(force)
        cost_ref[...] = jnp.zeros_like(cost_ref)

    lane = lax.broadcasted_iota(jnp.int32, (levels + 3, 128), 1)

    for half in range(2):
        xs = [rec_ref[half * 8 + i] for i in range(8)]
        for d in (1, 2, 4):
            keep = (lane // (16 * d)) % 2 == 0
            new = list(xs)
            for i in range(8):
                if i & d == 0:
                    lo, hi = xs[i], xs[i + d]
                    new[i] = jnp.where(keep, lo, pltpu.roll(hi, 16 * d, axis=1))
                    new[i + d] = jnp.where(keep, pltpu.roll(lo, 128 - 16 * d, axis=1), hi)
            xs = new
        for i in range(8):
            tiles[i, 0 : levels + 3, half * 128 : half * 128 + 128] = xs[i]

    iota8 = lax.broadcasted_iota(jnp.int32, (8, 256), 0)

    def tile(q, _):
        value = tiles[q, levels : levels + 1, :]
        inverse = tiles[q, levels + 1 : levels + 2, :]
        cell = tiles[q, levels + 2 : levels + 3, :].astype(jnp.int32)
        row = cell >> 7
        col = cell & 127
        part = row >> 5
        block = (row >> 3) & 3
        group = 2 * block + part
        valid = inverse > 0.0
        gmin = jnp.min(jnp.where(valid, group, 8))
        gmax = jnp.max(jnp.where(valid, group, -1))
        rmask = iota8 == (row & 7)
        iota128 = lax.broadcasted_iota(jnp.int32, (128, 256), 0)
        pick = jnp.where(iota128 == col, 1.0, 0.0).astype(BF16)
        pick2 = jnp.concatenate([pick, pick], axis=0)

        def sample(g, acc):
            s = jnp.dot(
                bgm_ref[pl.ds(pl.multiple_of(g * rows_in, 16), rows_in), :],
                pick2,
                preferred_element_type=F32,
            )
            parts = [jnp.zeros((8, 256), F32) for _ in range(4)]
            for k in range(levels):
                parts[k % 4] = parts[k % 4] + tiles[q, k : k + 1, :] * s[8 * k : 8 * k + 8, :]
            total = (parts[0] + parts[1]) + (parts[2] + parts[3])
            return acc + jnp.where(group == g, total, 0.0)

        acc = lax.fori_loop(gmin, gmax + 1, sample, jnp.zeros((8, 256), F32))
        equiv = jnp.sum(jnp.where(rmask, acc, 0.0), axis=0, keepdims=True)
        scaled = (value - equiv) * inverse
        magnitude = jnp.abs(scaled)
        cost_ref[...] += jnp.where(
            magnitude <= HUBER_EDGE,
            0.5 * scaled * scaled,
            HUBER_EDGE * magnitude - 0.5 * HUBER_EDGE * HUBER_EDGE,
        )
        response = HUBER_EDGE / jnp.maximum(magnitude, HUBER_EDGE) * scaled * inverse
        wr = tiles[q, 0:levels, :] * response
        hi = wr.astype(BF16).astype(F32)
        whi[0:levels, :] = hi
        wlo[0:levels, :] = wr - hi
        iota256 = lax.broadcasted_iota(jnp.int32, (256, 256), 0)
        place = jnp.where(iota256 == col + 128 * part, 1.0, 0.0).astype(BF16)
        place2 = jnp.concatenate([place, place], axis=1)

        def spread(b, _):
            m = jnp.where(rmask & (block == b), 1.0, 0.0)
            for k in range(0, levels, 2):
                for half, src in ((0, whi), (256, wlo)):
                    x = jnp.concatenate([m * src[k : k + 1, :], m * src[k + 1 : k + 2, :]], axis=0)
                    amat[8 * k : 8 * k + 16, half : half + 256] = x.astype(BF16)
            at = pl.ds(pl.multiple_of(b * rows_in, 8), rows_in)
            force[at, :] += lax.dot_general(
                amat[...], place2, (((1,), (1,)), ((), ())), preferred_element_type=F32
            )
            return 0

        lax.fori_loop(gmin >> 1, (gmax >> 1) + 1, spread, 0)
        return 0

    lax.fori_loop(0, 8, tile, 0)

    @pl.when(step == steps - 1)
    def _():
        for b in range(4):
            for part in range(2):
                r0 = 32 * part + 8 * b
                sea = sea_ref[r0 : r0 + 8, :].astype(F32)

                def body(k, _):
                    f = force[pl.ds(pl.multiple_of(b * rows_in + 8 * k, 8), 8), 128 * part : 128 * part + 128]
                    state_ref[k, r0 : r0 + 8, :] = sea * es_ref[k, r0 : r0 + 8, :] * f
                    return 0

                lax.fori_loop(0, levels, body, 0, unroll=5)


def edges(x_ref, east_ref, west_ref):
    ny = x_ref.shape[1]
    nx = x_ref.shape[2]

    def body(k, _):
        x = x_ref[k]
        t = jnp.transpose(x)
        pad = jnp.zeros((8, nx - ny), F32)
        last = jnp.concatenate([t[nx - 8 : nx, :], pad], axis=1)
        sub = lax.broadcasted_iota(jnp.int32, (8, nx), 0)
        top = pltpu.roll(x[ny - 8 : ny, :], 4, axis=0)
        east_ref[k] = jnp.where(sub < 4, top, last)
        west_ref[k] = jnp.concatenate([t[0:8, :], pad], axis=1)
        return 0

    lax.fori_loop(0, x_ref.shape[0], body, 0)


def assemble(info_ref, x_ref, fw_ref, fe_ref, side_ref, one_ref, two_ref):
    levels, ny, nx = x_ref.shape
    shift = info_ref[0]
    even = info_ref[1]
    fold = info_ref[2]
    lane = lax.broadcasted_iota(jnp.int32, (8, 128), 1)
    rel_a = shift + 3 - lane
    rel_b = jnp.where(lane < 64, shift + 3 - 128 - lane, shift + 3 + 128 - lane)

    def mirror(west, own, east, rel):
        idx = rel & 127
        w = jnp.take_along_axis(west, idx, axis=1)
        o = jnp.take_along_axis(own, idx, axis=1)
        e = jnp.take_along_axis(east, idx, axis=1)
        return jnp.where(rel < 0, w, jnp.where(rel < 128, o, e))

    def body(k, _):
        fw = fw_ref[k]
        fe = fe_ref[k]
        wt = jnp.concatenate([fw, jnp.zeros((nx - 8, nx), F32)], axis=0)
        et = jnp.concatenate([fe, jnp.zeros((nx - 8, nx), F32)], axis=0)
        full = jnp.concatenate([fe, jnp.zeros((nx - 16, nx), F32), fw], axis=0)
        side = jnp.transpose(full)[0:ny, :]
        side_ref[k] = side
        top_a = pltpu.roll(x_ref[k, ny - 8 : ny, :], 4, axis=0)[0:4, :]
        top_b = pltpu.roll(side[ny - 8 : ny, :], 4, axis=0)[0:4, :]
        bot_a = x_ref[k, 0:8, :][0:4, :]
        bot_b = side[0:8, :][0:4, :]
        own8 = x_ref[k, ny - 8 : ny, :]
        east8 = side[ny - 8 : ny, :]
        west8 = pltpu.roll(fw, 4, axis=0)
        fold_a = mirror(west8, own8, east8, rel_a)
        fold_b = mirror(west8, own8, east8, rel_b)

        @pl.when(even == 1)
        def _():
            one_ref[k, :, 0:nx] = top_a
            one_ref[k, :, nx : 2 * nx] = top_b
            two_ref[k, :, 0:nx] = bot_a
            two_ref[k, :, nx : 2 * nx] = bot_b

        @pl.when(even == 0)
        def _():
            one_ref[k, :, 0:nx] = bot_a
            one_ref[k, :, nx : 2 * nx] = bot_b

            @pl.when(fold == 0)
            def _():
                two_ref[k, :, 0:nx] = top_a
                two_ref[k, :, nx : 2 * nx] = top_b

            @pl.when(fold == 1)
            def _():
                for d in range(4):
                    two_ref[k, d : d + 1, 0:nx] = fold_a[7 - d : 8 - d, :]
                    two_ref[k, d : d + 1, nx : 2 * nx] = fold_b[7 - d : 8 - d, :]

        return 0

    lax.fori_loop(0, levels, body, 0)


def diffuse(info_ref, x_ref, side_ref, one_ref, two_ref, cx_ref, cside_ref, cone_ref, ctwo_ref, es_ref, out_ref, coef):
    ny, nx = x_ref.shape[1], x_ref.shape[2]
    even = info_ref[1]

    def halo_rows(one, two):
        return jnp.where(
            even == 1,
            jnp.concatenate([one, two], axis=0),
            jnp.concatenate([two, one], axis=0),
        )

    def whole(k, x, side, one, two):
        left = jnp.concatenate([x[k], side[k]], axis=1)
        return jnp.concatenate([left, halo_rows(one[k], two[k])], axis=0)

    rows = ny + 8
    cols = 2 * nx

    @pl.when(pl.program_id(0) == 0)
    def _():
        col = lax.broadcasted_iota(jnp.int32, (rows, cols), 1)
        live = (col < nx + 4) | (col >= cols - 4)
        east = whole(0, cx_ref, cside_ref, cone_ref, ctwo_ref)
        north = whole(1, cx_ref, cside_ref, cone_ref, ctwo_ref)
        sea = whole(2, cx_ref, cside_ref, cone_ref, ctwo_ref)
        sea = jnp.where(live, sea, 0.0)
        east = jnp.where(live, east, 0.0) * sea
        north = jnp.where(live, north, 0.0) * sea
        a_e = east * pltpu.roll(sea, cols - 1, axis=1)
        a_w = east * pltpu.roll(sea, 1, axis=1)
        a_n = north * pltpu.roll(sea, rows - 1, axis=0)
        a_s = north * pltpu.roll(sea, 1, axis=0)
        coef[0] = 1.0 - ((a_e + a_w) + (a_n + a_s))
        coef[1] = a_e
        coef[2] = a_w
        coef[3] = a_n
        coef[4] = a_s

    def body(k, _):
        s = whole(k, x_ref, side_ref, one_ref, two_ref)
        for _ in range(STEPS):
            s = (
                coef[0] * s
                + (coef[1] * pltpu.roll(s, cols - 1, axis=1) + coef[2] * pltpu.roll(s, 1, axis=1))
                + (coef[3] * pltpu.roll(s, rows - 1, axis=0) + coef[4] * pltpu.roll(s, 1, axis=0))
            )
        out_ref[k] = es_ref[k] * s[0:ny, 0:nx]
        return 0

    lax.fori_loop(0, x_ref.shape[0], body, 0)


def vmem():
    return pl.BlockSpec(memory_space=pltpu.VMEM)


def smem():
    return pl.BlockSpec(memory_space=pltpu.SMEM)


def params():
    return pltpu.CompilerParams(vmem_limit_bytes=VMEM_LIMIT)


def perm_of(n_lat, n_lon, rule):
    pairs = []
    for a in range(n_lat):
        for b in range(n_lon):
            to = rule(a, b)
            if to is not None:
                pairs.append((a * n_lon + b, to[0] * n_lon + to[1] % n_lon))
    return pairs


def exchange(x, info, turn):
    levels, ny, nx = x.shape
    n_lat = lax.axis_size("lat")
    n_lon = lax.axis_size("lon")
    msg = jax.ShapeDtypeStruct((levels, 8, nx), F32)
    to_east, to_west = pl.pallas_call(
        edges,
        out_shape=(msg, msg),
        in_specs=[vmem()],
        out_specs=(vmem(), vmem()),
        compiler_params=params(),
        cost_estimate=pl.CostEstimate(flops=levels * 1000, bytes_accessed=levels * 40000, transcendentals=0),
        name="edges",
    )(x)
    from_west = lax.ppermute(to_east, "lon", [(i, (i + 1) % n_lon) for i in range(n_lon)])
    from_east = lax.ppermute(to_west, "lon", [((i + 1) % n_lon, i) for i in range(n_lon)])
    rows = jax.ShapeDtypeStruct((levels, 4, 2 * nx), F32)
    side, one, two = pl.pallas_call(
        assemble,
        out_shape=(jax.ShapeDtypeStruct(x.shape, F32), rows, rows),
        in_specs=[smem(), vmem(), vmem(), vmem()],
        out_specs=(vmem(), vmem(), vmem()),
        compiler_params=params(),
        cost_estimate=pl.CostEstimate(flops=levels * 1000, bytes_accessed=levels * 80000, transcendentals=0),
        name="assemble",
    )(info, x, from_west, from_east)
    got_one = lax.ppermute(one, ("lat", "lon"), perm_of(n_lat, n_lon, lambda a, b: (a ^ 1, b)))

    def branch(q):
        def rule(a, b):
            if a == n_lat - 1:
                return (a, q - b)
            if a == 0:
                return None
            return (((a + 1) ^ 1) - 1, b)

        return lambda v: lax.ppermute(v, ("lat", "lon"), perm_of(n_lat, n_lon, rule))

    got_two = lax.switch(turn, [branch(q) for q in range(n_lon)], two)
    return side, got_one, got_two


def shards(
    background,
    error_scale,
    east_rate,
    north_rate,
    sea_mask,
    partner,
    obs_weight,
    obs_value,
    obs_error,
    obs_column,
    obs_count,
):
    levels = background.shape[0] * background.shape[1]
    ny = background.shape[2]
    nx = background.shape[3]
    capacity = obs_weight.shape[3]
    owners = obs_weight.shape[1]
    n_lat = lax.axis_size("lat")
    n_lon = lax.axis_size("lon")
    lat_at = lax.axis_index("lat").astype(jnp.int32)

    slot_index = lax.broadcasted_iota(jnp.int32, (owners, capacity), 1)
    valid_slot = slot_index < obs_count[0][:, None]
    inverse = jnp.where(valid_slot, 1.0 / obs_error[0], 0.0)
    packed = jnp.concatenate(
        [
            obs_weight[0],
            obs_value[0][:, None, :],
            inverse[:, None, :],
            obs_column[0].astype(F32)[:, None, :],
        ],
        axis=1,
    )
    received = lax.all_to_all(packed, ("lat", "lon"), split_axis=0, concat_axis=0, tiled=True)

    moved = (partner[0] - 3) % (nx * n_lon)
    turn = moved // nx
    info = jnp.stack([moved % nx, 1 - lat_at % 2, (lat_at == n_lat - 1).astype(jnp.int32), turn]).astype(jnp.int32)
    coefs = jnp.stack([east_rate, north_rate, sea_mask.astype(F32)])
    cside, cone, ctwo = exchange(coefs, info, turn)

    bg = background.reshape(levels, ny, nx)
    es = error_scale.reshape(levels, ny, nx)
    bgm = pl.pallas_call(
        split_background,
        out_shape=jax.ShapeDtypeStruct((8 * levels * 8, 256), BF16),
        in_specs=[vmem()],
        out_specs=vmem(),
        compiler_params=params(),
        cost_estimate=pl.CostEstimate(flops=3000000, bytes_accessed=3300000, transcendentals=0),
        name="split_background",
    )(bg)

    per = 16
    state, cost = pl.pallas_call(
        observe,
        grid=(owners // per,),
        out_shape=(
            jax.ShapeDtypeStruct((levels, ny, nx), F32),
            jax.ShapeDtypeStruct((1, 256), F32),
        ),
        in_specs=[
            pl.BlockSpec((per, levels + 3, capacity), lambda i: (i, 0, 0)),
            pl.BlockSpec((64 * levels, 256), lambda i: (0, 0)),
            pl.BlockSpec((ny, nx), lambda i: (0, 0)),
            pl.BlockSpec((levels, ny, nx), lambda i: (0, 0, 0)),
        ],
        out_specs=(
            pl.BlockSpec((levels, ny, nx), lambda i: (0, 0, 0)),
            pl.BlockSpec((1, 256), lambda i: (0, 0)),
        ),
        scratch_shapes=[
            pltpu.VMEM((8, 56, 256), F32),
            pltpu.VMEM((32 * levels, 256), F32),
            pltpu.VMEM((56, 256), F32),
            pltpu.VMEM((56, 256), F32),
            pltpu.VMEM((8 * levels, 512), BF16),
        ],
        compiler_params=params(),
        name="observe",
    )(received, bgm, sea_mask, es)

    share = jnp.sum(cost)
    shares = lax.all_to_all(
        jnp.broadcast_to(share, (owners, 1, 128)), ("lat", "lon"), split_axis=0, concat_axis=0, tiled=True
    )
    cost_share = jnp.sum(shares[:, 0, 0]) / (owners * owners * capacity)

    side, one, two = exchange(state, info, turn)

    blk = 5
    lev = lambda i: (i, 0, 0)
    fix = lambda i: (0, 0, 0)
    increment = pl.pallas_call(
        diffuse,
        grid=(levels // blk,),
        out_shape=jax.ShapeDtypeStruct((levels, ny, nx), F32),
        in_specs=[
            smem(),
            pl.BlockSpec((blk, ny, nx), lev),
            pl.BlockSpec((blk, ny, nx), lev),
            pl.BlockSpec((blk, 4, 2 * nx), lev),
            pl.BlockSpec((blk, 4, 2 * nx), lev),
            pl.BlockSpec((3, ny, nx), fix),
            pl.BlockSpec((3, ny, nx), fix),
            pl.BlockSpec((3, 4, 2 * nx), fix),
            pl.BlockSpec((3, 4, 2 * nx), fix),
            pl.BlockSpec((blk, ny, nx), lev),
        ],
        out_specs=pl.BlockSpec((blk, ny, nx), lev),
        scratch_shapes=[pltpu.VMEM((5, ny + 8, 2 * nx), F32)],
        compiler_params=params(),
        name="diffuse",
    )(info, state, side, one, two, coefs, cside, cone, ctwo, es)
    return (increment.reshape(background.shape), cost_share)


def solution(mesh):
    in_specs = (
        P(None, None, "lat", "lon"),
        P(None, None, "lat", "lon"),
        P("lat", "lon"),
        P("lat", "lon"),
        P("lat", "lon"),
        P(),
        P(("lat", "lon"), None, None, None),
        P(("lat", "lon"), None, None),
        P(("lat", "lon"), None, None),
        P(("lat", "lon"), None, None),
        P(("lat", "lon"), None),
    )
    out_specs = (P(None, None, "lat", "lon"), P())
    return jax.shard_map(shards, mesh=mesh, in_specs=in_specs, out_specs=out_specs, check_vma=False)
```

time: 597 us -> 381 us (0.64); the launches traced: 588 us -> 380 us
  Pallas kernels: 0 us -> 269 us
  blocking collectives: 217 us -> 0 us
  other arithmetic: 184 us -> 5.76 us
  local copies, waits for them, and re-layouts: 117 us -> 9.53 us
  waiting for transfers between devices: 4.51 us -> 52.7 us
  starting transfers between devices: 61.5 us -> 39.1 us
    pallas_call x0 -> x7, Pallas kernels: none -> 269 us  [the longest x1 221 us: shards(): pl.pallas_call(observe, grid=(owners // per,), out_shape=(jax.ShapeDtypeS...]
    all_gather x5 -> x0, blocking collectives: 153 us -> none  [extend(): lax.all_gather(field_in[:, field_in.shape[1] - rim_depth:, :], 'lon', axi...]
    scatter-add x1 -> x0, other arithmetic: 89.8 us -> none  [shards(): forcing = jnp.zeros((levels, lat_cells * lon_cells), jnp.float32).at[:, c...]
    gather x8 -> x0, local copies, waits for them, and re-layouts: 69.4 us -> none  [the longest x2 63.4 us: shards(): sampled = flat_bg[:, cells_in]]
    psum x1 -> x0, blocking collectives: 64.6 us -> none  [shards(): lax.psum(jnp.sum(huber_terms), ('lat', 'lon'))]
    all_to_all x1, waiting for transfers between devices: 0.01 us -> 39.7 us  [shards(): lax.all_to_all(packed, ('lat', 'lon'), split_axis=0, concat_axis=0, tiled...]
    ppermute x20 -> x8, starting transfers between devices: 50.6 us -> 19.6 us  [the longest x2 10.3 us: exchange(): lax.ppermute(to_west, 'lon', [((i + 1) % n_lon, i) for i in range(n_lon)])]
    add x3 -> x0, other arithmetic: 29.6 us -> none  [relax(): return center + sea_here * (east_here * along_term + north_here * across)]
  transfers between devices with their start and end apart: 21 -> 10, of which waited for: 2 -> 4; matrix products, arithmetic and copies ran while one was open for 6% -> 2% of each run, Pallas kernels for 0% -> 5%
where the time goes in v1:
time: 381 us; the launch traced here: 380 us
  Pallas kernels  269 us (71%)
  waiting for transfers between devices  52.7 us (14%)
  starting transfers between devices  39.1 us (10%)
  local copies, waits for them, and re-layouts  9.53 us (3%)
  other arithmetic  5.76 us (2%)
    pallas_call x1, Pallas kernels, shards(): pl.pallas_call(observe, grid=(owners // per,), out_shape=(jax.ShapeDtypeS...  221 us
    all_to_all x1, waiting for transfers between devices, shards(): lax.all_to_all(packed, ('lat', 'lon'), split_axis=0, concat_axis=0, tiled...  39.7 us
    pallas_call x1, Pallas kernels, shards(): pl.pallas_call(diffuse, grid=(levels // blk,), out_shape=jax.ShapeDtypeSt...  22.8 us
    pallas_call x2, Pallas kernels, exchange(): pl.pallas_call(assemble, out_shape=(jax.ShapeDtypeStruct(x.shape, F32), r...  12.9 us
    ppermute x2, waiting for transfers between devices, branch(): lax.ppermute(v, ('lat', 'lon'), perm_of(n_lat, n_lon, rule))  11.4 us
    all_to_all x1, starting transfers between devices, shards(): lax.all_to_all(packed, ('lat', 'lon'), split_axis=0, concat_axis=0, tiled...  10.9 us
    ppermute x2, starting transfers between devices, exchange(): lax.ppermute(to_west, 'lon', [((i + 1) % n_lon, i) for i in range(n_lon)])  10.3 us
    pallas_call x2, Pallas kernels, exchange(): pl.pallas_call(edges, out_shape=(msg, msg), in_specs=[vmem()], out_specs=...  9.06 us
  transfers between devices with their start and end apart: 10, of which 4 were waited for; matrix products, arithmetic and copies ran while one was open for 2% of the time, Pallas kernels for 5%

profile of v1, /device:TPU:6, one launch (start us, length us, event | category | flops | bytes accessed | tf_op | source)
XLA Modules:
  0.0 379.5 jit_solution(5288673898231949185)
XLA Ops:
  0.7 3.9 %copy.19 = f32[1,128,50,128]{3,2,1,0:T(8,128)S(1)} copy(f32[1,128,50,128]{3,1,2,0:T(8,128)} %param.49) | data formatting | bytes 6553600 | tf_op args[6]
  4.9 2.2 pad_maximum_fusion
  7.1 10.9 %all-to-all-start = ((f32[128,53,128]{2,1,0:T(8,128)}), f32[128,53,128]{2,1,0:T(8,128)}, u32[]{:S(2)}, u32[]{:S(2)}) async-start(f32[128,53,128]{2,1,0:T(8,128)} %pad_maximum_fusion), calls=%async_computation | async-start | bytes 7340032 | tf_op jit(solution)/shard_map/all_to_all | solution.py:375
  19.9 3.1 split_background.1.bgm_ref
  23.6 39.7 %all-to-all-done.rec_ref = f32[128,53,128]{2,1,0:T(8,128)} async-done(((f32[128,53,128]{2,1,0:T(8,128)}), f32[128,53,128]{2,1,0:T(8,128)}, u32[]{:S(2)}, u32[]{:S(2)}) %all-to-all-start) | async-done | bytes 3473440 | tf_op jit(solution)/shard_map/all_to_all | solution.py:375
  63.3 221.3 %observe.1 = (f32[50,64,128]{2,1,0:T(8,128)}, f32[1,256]{1,0:T(1,128)}) custom-call(f32[128,53,128]{2,1,0:T(8,128)} %all-to-all-done.rec_ref, bf16[3200,256]{1,0:T(8,128)(2,1)} %split_background.1.bgm_ref, s32[64,128]{1,0:T(8,128)} %sea_ref.1, f32[50,64,128]{2,1,0:T(8,128)} %bitcast.20), custom_call_target="tpu_custom_call" | custom-call | tf_op jit(solution)/shard_map/observe/pallas_call | solution.py:396
  284.7 7.3 %edges.2 = (f32[50,8,128]{2,1,0:T(8,128)}, f32[50,8,128]{2,1,0:T(8,128)}) custom-call(f32[50,64,128]{2,1,0:T(8,128)} %get-tuple-element.80.x_ref), custom_call_target="tpu_custom_call" | custom-call | flops 50000 | bytes 2000000 | tf_op jit(solution)/shard_map/edges/pallas_call | solution.py:304
  292.4 4.9 %collective-permute-start.33 = (f32[50,8,128]{2,1,0:T(8,128)}, f32[50,8,128]{2,1,0:T(8,128)S(1)}, u32[]{:S(2)}, u32[]{:S(2)}) collective-permute-start(f32[50,8,128]{2,1,0:T(8,128)} %get-tuple-element.82), channel_id=1, source_target_pairs={{1,0},{2,1},{3,2},{4,3},{5,4},{6,5},{7,6},{8,7},{9,8},{10,9},{11,1... | collective-permute-start | bytes 614408 | tf_op jit(solution)/shard_map/ppermute | solution.py:314
  297.3 1.3 reduce_sum.18
  298.6 1.2 broadcast_in_dim.10
  299.8 8.6 %all-to-all-start.1 = ((f32[128,1,128]{2,1,0:T(1,128)}), f32[128,1,128]{2,1,0:T(1,128)S(1)}, u32[]{:S(2)}, u32[]{:S(2)}) async-start(f32[128,1,128]{2,1,0:T(1,128)} %broadcast_in_dim.10), calls=%async_computation.1 | async-start | bytes 131072 | tf_op jit(solution)/shard_map/all_to_all | solution.py:425
  309.8 10.8 %assemble.2 = (f32[50,64,128]{2,1,0:T(8,128)}, f32[50,4,256]{2,1,0:T(4,128)}, f32[50,4,256]{2,1,0:T(4,128)S(1)}) custom-call(s32[4]{0:T(128)} %pad_add_fusion.info_ref, f32[50,64,128]{2,1,0:T(8,128)} %get-tuple-element.80.x_ref, f32[50,8,128]{2,1,0:T(8,128)} %copy-done, f32[50,8,128]{2,1,0:T(8,128)} %copy-done.1), custom_call_target="tpu_custom_call" | custom-call | flops 50000 | bytes 4000000 | tf_op jit(solution)/shard_map/assemble/pallas_call | solution.py:316
  322.0 1.8 edges.3
  323.8 5.4 %collective-permute-start.36 = (f32[3,8,128]{2,1,0:T(8,128)}, f32[3,8,128]{2,1,0:T(8,128)S(1)}, u32[]{:S(2)}, u32[]{:S(2)}) collective-permute-start(f32[3,8,128]{2,1,0:T(8,128)} %get-tuple-element.87), channel_id=1, source_target_pairs={{1,0},{2,1},{3,2},{4,3},{5,4},{6,5},{7,6},{8,7},{9,8},{10,9},{11,1... | collective-permute-start | bytes 36872 | tf_op jit(solution)/shard_map/ppermute | solution.py:314
  329.2 1.6 collective-permute-done.35.fw_ref
  332.0 2.0 assemble.3
  334.0 1.2 collective-permute-start.37
  335.2 7.8 %conditional.3 = (f32[3,4,256]{2,1,0:T(4,128)}) conditional(s32[]{:T(128)} %clamp.4, f32[3,4,256]{2,1,0:T(4,128)S(1)} %get-tuple-element.90, f32[3,4,256]{2,1,0:T(4,128)S(1)} %get-tuple-element.90, f32[3,4,256]{2,1,0:T(4,128)S(1)} %get-tuple-element.90, f32[3,4,256]{2,1,0:T(4,128)S(1)} %get-tuple-element.90, ...), branch_computations={%region_16.17_spmd, %region_17.18_spmd, %region_18.19_spmd, %regio... | conditional | bytes 49200 | solution.py:337
  335.2 3.4 collective-permute-start.17
  338.7 4.4 %collective-permute-done.17 = f32[3,4,256]{2,1,0:T(4,128)} collective-permute-done((f32[3,4,256]{2,1,0:T(4,128)S(1)}, f32[3,4,256]{2,1,0:T(4,128)}, u32[]{:S(2)}, u32[]{:S(2)}) %collective-permute-start.17) | collective-permute-done | bytes 12320 | tf_op jit(solution)/shard_map/cond/branch_1_fun/ppermute | solution.py:335
  344.4 10.5 %conditional.2 = (f32[50,4,256]{2,1,0:T(4,128)}) conditional(s32[]{:T(128)} %clamp.4, f32[50,4,256]{2,1,0:T(4,128)S(1)} %get-tuple-element.85, f32[50,4,256]{2,1,0:T(4,128)S(1)} %get-tuple-element.85, f32[50,4,256]{2,1,0:T(4,128)S(1)} %get-tuple-element.85, f32[50,4,256]{2,1,0:T(4,128)S(1)} %get-tuple-element.85, ...), branch_computations={%region_0.1_spmd, %region_1.2_spmd, %region_2.3_spmd, %region_3.4_... | conditional | bytes 819248 | solution.py:337
  344.4 3.4 collective-permute-start.1
  347.9 7.0 %collective-permute-done.1 = f32[50,4,256]{2,1,0:T(4,128)} collective-permute-done((f32[50,4,256]{2,1,0:T(4,128)S(1)}, f32[50,4,256]{2,1,0:T(4,128)}, u32[]{:S(2)}, u32[]{:S(2)}) %collective-permute-start.1) | collective-permute-done | bytes 204832 | tf_op jit(solution)/shard_map/cond/branch_1_fun/ppermute | solution.py:335
  355.6 22.8 %diffuse.1 = f32[50,64,128]{2,1,0:T(8,128)} custom-call(s32[4]{0:T(128)} %pad_add_fusion.info_ref, f32[50,64,128]{2,1,0:T(8,128)} %get-tuple-element.80.x_ref, f32[50,64,128]{2,1,0:T(8,128)} %get-tuple-element.83.side_ref, f32[50,4,256]{2,1,0:T(4,128)} %copy-done.2, f32[50,4,256]{2,1,0:T(4,128)} %get-tuple-element.92.two_ref, ...), custom_call_target="tpu_custom_call" | custom-call | tf_op jit(solution)/shard_map/diffuse/pallas_call | solution.py:435
  (43 shorter events, 8.0 us)
Async XLA Ops:
  0.6 4.0 %copy-start.5 = (f32[1,128,128]{2,1,0:T(8,128)S(1)}, f32[1,128,128]{2,1,0:T(8,128)}, u32[]{:S(2)}) copy-start(f32[1,128,128]{2,1,0:T(8,128)} %param.51) | copy-start | bytes 196612
  0.6 4.0 %copy-start.6 = (s32[1,128,128]{2,1,0:T(8,128)S(1)}, s32[1,128,128]{2,1,0:T(8,128)}, u32[]{:S(2)}) copy-start(s32[1,128,128]{2,1,0:T(8,128)} %param.52) | copy-start | bytes 196612
  0.7 4.0 %copy-start.12 = (s32[1,128]{1,0:T(1,128)S(1)}, s32[1,128]{1,0:T(1,128)}, u32[]{:S(2)}) copy-start(s32[1,128]{1,0:T(1,128)} %param.53) | copy-start | bytes 1540
  0.7 4.2 %copy-start.4 = (f32[1,128,128]{2,1,0:T(8,128)S(1)}, f32[1,128,128]{2,1,0:T(8,128)}, u32[]{:S(2)}) copy-start(f32[1,128,128]{2,1,0:T(8,128)} %param.50) | copy-start | bytes 196612
  7.1 56.2 %all-to-all-start = ((f32[128,53,128]{2,1,0:T(8,128)}), f32[128,53,128]{2,1,0:T(8,128)}, u32[]{:S(2)}, u32[]{:S(2)}) async-start(f32[128,53,128]{2,1,0:T(8,128)} %pad_maximum_fusion), calls=%async_computation | async-start | bytes 7340032 | tf_op jit(solution)/shard_map/all_to_all | solution.py:375
  63.3 233.9 %copy-start.3 = (s32[64,128]{1,0:T(8,128)S(1)}, s32[64,128]{1,0:T(8,128)}, u32[]{:S(2)}) copy-start(s32[64,128]{1,0:T(8,128)} %sea_ref.1) | copy-start | bytes 98308
  284.7 36.7 %copy-start.7 = (f32[64,128]{1,0:T(8,128)S(1)}, f32[64,128]{1,0:T(8,128)}, u32[]{:S(2)}) copy-start(f32[64,128]{1,0:T(8,128)} %param.46) | copy-start | bytes 98308
  284.7 36.7 %copy-start.8 = (f32[64,128]{1,0:T(8,128)S(1)}, f32[64,128]{1,0:T(8,128)}, u32[]{:S(2)}) copy-start(f32[64,128]{1,0:T(8,128)} %param.45) | copy-start | bytes 98308
  291.9 16.5 %collective-permute-start.32 = (f32[50,8,128]{2,1,0:T(8,128)}, f32[50,8,128]{2,1,0:T(8,128)S(1)}, u32[]{:S(2)}, u32[]{:S(2)}) collective-permute-start(f32[50,8,128]{2,1,0:T(8,128)} %get-tuple-element.81), channel_id=1, source_target_pairs={{0,1},{1,2},{2,3},{3,4},{4,5},{5,6},{6,7},{7,8},{8,9},{9,10},{10,1... | collective-permute-start | bytes 614408 | tf_op jit(solution)/shard_map/ppermute | solution.py:313
  292.4 16.0 %collective-permute-start.33 = (f32[50,8,128]{2,1,0:T(8,128)}, f32[50,8,128]{2,1,0:T(8,128)S(1)}, u32[]{:S(2)}, u32[]{:S(2)}) collective-permute-start(f32[50,8,128]{2,1,0:T(8,128)} %get-tuple-element.82), channel_id=1, source_target_pairs={{1,0},{2,1},{3,2},{4,3},{5,4},{6,5},{7,6},{8,7},{9,8},{10,9},{11,1... | collective-permute-start | bytes 614408 | tf_op jit(solution)/shard_map/ppermute | solution.py:314
  299.8 43.3 %all-to-all-start.1 = ((f32[128,1,128]{2,1,0:T(1,128)}), f32[128,1,128]{2,1,0:T(1,128)S(1)}, u32[]{:S(2)}, u32[]{:S(2)}) async-start(f32[128,1,128]{2,1,0:T(1,128)} %broadcast_in_dim.10), calls=%async_computation.1 | async-start | bytes 131072 | tf_op jit(solution)/shard_map/all_to_all | solution.py:425
  308.4 0.7 copy-start
  309.1 0.7 copy-start.1
  320.6 34.4 %collective-permute-start.34 = (f32[50,4,256]{2,1,0:T(4,128)}, f32[50,4,256]{2,1,0:T(4,128)S(1)}, u32[]{:S(2)}, u32[]{:S(2)}) collective-permute-start(f32[50,4,256]{2,1,0:T(4,128)} %get-tuple-element.84), channel_id=1, source_target_pairs={{0,16},{1,17},{2,18},{3,19},{4,20},{5,21},{6,22},{7,23},{8,24},{9,... | collective-permute-start | bytes 614408 | tf_op jit(solution)/shard_map/ppermute | solution.py:325
  323.8 6.9 %collective-permute-start.35 = (f32[3,8,128]{2,1,0:T(8,128)}, f32[3,8,128]{2,1,0:T(8,128)S(1)}, u32[]{:S(2)}, u32[]{:S(2)}) collective-permute-start(f32[3,8,128]{2,1,0:T(8,128)} %get-tuple-element.86), channel_id=1, source_target_pairs={{0,1},{1,2},{2,3},{3,4},{4,5},{5,6},{6,7},{7,8},{8,9},{9,10},{10,1... | collective-permute-start | bytes 36872 | tf_op jit(solution)/shard_map/ppermute | solution.py:313
  323.8 7.0 %collective-permute-start.36 = (f32[3,8,128]{2,1,0:T(8,128)}, f32[3,8,128]{2,1,0:T(8,128)S(1)}, u32[]{:S(2)}, u32[]{:S(2)}) collective-permute-start(f32[3,8,128]{2,1,0:T(8,128)} %get-tuple-element.87), channel_id=1, source_target_pairs={{1,0},{2,1},{3,2},{4,3},{5,4},{6,5},{7,6},{8,7},{9,8},{10,9},{11,1... | collective-permute-start | bytes 36872 | tf_op jit(solution)/shard_map/ppermute | solution.py:314
  330.8 0.6 copy-start.10
  331.4 0.6 copy-start.11
  334.0 20.9 %collective-permute-start.37 = (f32[3,4,256]{2,1,0:T(4,128)}, f32[3,4,256]{2,1,0:T(4,128)S(1)}, u32[]{:S(2)}, u32[]{:S(2)}) collective-permute-start(f32[3,4,256]{2,1,0:T(4,128)} %get-tuple-element.89), channel_id=1, source_target_pairs={{0,16},{1,17},{2,18},{3,19},{4,20},{5,21},{6,22},{7,23},{8,24},{9,... | collective-permute-start | bytes 36872 | tf_op jit(solution)/shard_map/ppermute | solution.py:325
  335.2 7.8 %collective-permute-start.17 = (f32[3,4,256]{2,1,0:T(4,128)S(1)}, f32[3,4,256]{2,1,0:T(4,128)}, u32[]{:S(2)}, u32[]{:S(2)}) collective-permute-start(f32[3,4,256]{2,1,0:T(4,128)S(1)} %param.17), channel_id=1, source_target_pairs={{16,32},{17,33},{18,34},{19,35},{20,36},{21,37},{22,38},{23,39},{2... | collective-permute-start | bytes 36872 | tf_op jit(solution)/shard_map/cond/branch_1_fun/ppermute | solution.py:335
  344.4 10.5 %collective-permute-start.1 = (f32[50,4,256]{2,1,0:T(4,128)S(1)}, f32[50,4,256]{2,1,0:T(4,128)}, u32[]{:S(2)}, u32[]{:S(2)}) collective-permute-start(f32[50,4,256]{2,1,0:T(4,128)S(1)} %param.1), channel_id=1, source_target_pairs={{16,32},{17,33},{18,34},{19,35},{20,36},{21,37},{22,38},{23,39},{2... | collective-permute-start | bytes 614408 | tf_op jit(solution)/shard_map/cond/branch_1_fun/ppermute | solution.py:335
  354.9 0.6 copy-start.9
  354.9 0.7 copy-start.2

commit v2 on v1

--- a/solution.py
+++ b/solution.py
@@ -10,6 +10,7 @@
 HUBER_EDGE = 1.5
 F32 = jnp.float32
 BF16 = jnp.bfloat16
+WIDE = 2048
 VMEM_LIMIT = 56 * 1024 * 1024
 
 
@@ -34,39 +35,109 @@
             lax.fori_loop(0, levels // 2, body, 0, unroll=5)
 
 
+def pack(count_ref, w_ref, value_ref, error_ref, cell_ref, out_ref, order_ref):
+    levels, some, n = w_ref.shape
+    owners = order_ref.shape[0]
+    lane8 = lax.broadcasted_iota(jnp.int32, (8, n), 1)
+
+    @pl.when(pl.program_id(0) == 0)
+    def _():
+        counts = jnp.transpose(jnp.broadcast_to(count_ref[...], (owners, n)))
+        lane = lax.broadcasted_iota(jnp.int32, (owners, n), 1)
+        cell = cell_ref[...]
+        row = cell >> 7
+        key = (((row >> 3) & 3) << 11) | ((row >> 5) << 10) | ((row & 7) << 7) | (cell & 127)
+        key = jnp.where(lane < counts, key, 8192)
+        x = (key * n + lane).astype(F32)
+        size = 2
+        while size <= n:
+            step = size // 2
+            while step >= 1:
+                first = (lane & step) == 0
+                other = jnp.where(first, pltpu.roll(x, n - step, axis=1), pltpu.roll(x, step, axis=1))
+                least = first == ((lane & size) == 0)
+                x = jnp.where(least, jnp.minimum(x, other), jnp.maximum(x, other))
+                step //= 2
+            size *= 2
+        order_ref[...] = x.astype(jnp.int32)
+
+    for o in range(0, some, 8):
+        at = pl.ds(pl.multiple_of(pl.program_id(0) * some + o, 8), 8)
+        packed = order_ref[at, :]
+        order = packed & (n - 1)
+        valid = packed < 8192 * n
+
+        def put(k, v):
+            out_ref[pl.ds(o * 56 + k, 8, stride=56), :] = v
+
+        for k in range(levels):
+            put(k, jnp.take_along_axis(w_ref[k, o : o + 8, :], order, axis=1))
+        put(levels, jnp.take_along_axis(value_ref[at, :], order, axis=1))
+        error = jnp.take_along_axis(error_ref[at, :], order, axis=1)
+        put(levels + 1, jnp.where(valid, 1.0 / error, 0.0))
+        put(levels + 2, jnp.take_along_axis(cell_ref[at, :], order, axis=1).astype(F32))
+        for k in range(levels + 3, 56):
+            put(k, jnp.zeros((8, n), F32))
+
+
+def pack_call(count, weight, value, error, column):
+    levels, owners, n = weight.shape
+    some = 16
+    return pl.pallas_call(
+        pack,
+        grid=(owners // some,),
+        out_shape=jax.ShapeDtypeStruct((owners * 56, n), F32),
+        in_specs=[
+            pl.BlockSpec((1, owners), lambda i: (0, 0)),
+            pl.BlockSpec((levels, some, n), lambda i: (0, i, 0)),
+            pl.BlockSpec((owners, n), lambda i: (0, 0)),
+            pl.BlockSpec((owners, n), lambda i: (0, 0)),
+            pl.BlockSpec((owners, n), lambda i: (0, 0)),
+        ],
+        out_specs=pl.BlockSpec((some * 56, n), lambda i: (i, 0)),
+        scratch_shapes=[pltpu.VMEM((owners, n), jnp.int32)],
+        compiler_params=params(),
+        name="pack",
+    )(count, weight, value, error, column)
+
+
 def observe(rec_ref, bgm_ref, sea_ref, es_ref, state_ref, cost_ref, tiles, force, whi, wlo, amat):
-    step = pl.program_id(0)
-    steps = pl.num_programs(0)
     levels = es_ref.shape[0]
+    sources = rec_ref.shape[0] // 56
     rows_in = 8 * levels
-
-    @pl.when(step == 0)
-    def _():
-        force[...] = jnp.zeros_like(force)
-        cost_ref[...] = jnp.zeros_like(cost_ref)
-
-    lane = lax.broadcasted_iota(jnp.int32, (levels + 3, 128), 1)
-
-    for half in range(2):
-        xs = [rec_ref[half * 8 + i] for i in range(8)]
-        for d in (1, 2, 4):
-            keep = (lane // (16 * d)) % 2 == 0
-            new = list(xs)
+    wide = whi.shape[1]
+    total = tiles.shape[2]
+
+    force[...] = jnp.zeros_like(force)
+    cost_ref[...] = jnp.zeros_like(cost_ref)
+
+    def regroup(eight, _):
+        lane = lax.broadcasted_iota(jnp.int32, (8, 128), 1)
+        for r in range(0, 56, 8):
+            xs = [rec_ref[pl.ds(pl.multiple_of((eight * 8 + i) * 56 + r, 8), 8), :] for i in range(8)]
+            for d in (1, 2, 4):
+                keep = (lane // (16 * d)) % 2 == 0
+                new = list(xs)
+                for i in range(8):
+                    if i & d == 0:
+                        lo, hi = xs[i], xs[i + d]
+                        new[i] = jnp.where(keep, lo, pltpu.roll(hi, 16 * d, axis=1))
+                        new[i + d] = jnp.where(keep, pltpu.roll(lo, 128 - 16 * d, axis=1), hi)
+                xs = new
             for i in range(8):
-                if i & d == 0:
-                    lo, hi = xs[i], xs[i + d]
-                    new[i] = jnp.where(keep, lo, pltpu.roll(hi, 16 * d, axis=1))
-                    new[i + d] = jnp.where(keep, pltpu.roll(lo, 128 - 16 * d, axis=1), hi)
-            xs = new
-        for i in range(8):
-            tiles[i, 0 : levels + 3, half * 128 : half * 128 + 128] = xs[i]
-
-    iota8 = lax.broadcasted_iota(jnp.int32, (8, 256), 0)
-
-    def tile(q, _):
-        value = tiles[q, levels : levels + 1, :]
-        inverse = tiles[q, levels + 1 : levels + 2, :]
-        cell = tiles[q, levels + 2 : levels + 3, :].astype(jnp.int32)
+                tiles[i, r : r + 8, pl.ds(pl.multiple_of(eight * 128, 128), 128)] = xs[i]
+        return 0
+
+    lax.fori_loop(0, sources // 8, regroup, 0)
+
+    iota8 = lax.broadcasted_iota(jnp.int32, (8, wide), 0)
+
+    def tile(t, _):
+        q = t // (total // wide)
+        at_r = pl.ds(pl.multiple_of((t % (total // wide)) * wide, wide), wide)
+        value = tiles[q, levels : levels + 1, at_r]
+        inverse = tiles[q, levels + 1 : levels + 2, at_r]
+        cell = tiles[q, levels + 2 : levels + 3, at_r].astype(jnp.int32)
         row = cell >> 7
         col = cell & 127
         part = row >> 5
@@ -76,9 +147,11 @@
         gmin = jnp.min(jnp.where(valid, group, 8))
         gmax = jnp.max(jnp.where(valid, group, -1))
         rmask = iota8 == (row & 7)
-        iota128 = lax.broadcasted_iota(jnp.int32, (128, 256), 0)
-        pick = jnp.where(iota128 == col, 1.0, 0.0).astype(BF16)
-        pick2 = jnp.concatenate([pick, pick], axis=0)
+        iota128 = lax.broadcasted_iota(jnp.int32, (128, wide), 0)
+        pick = jnp.where(iota128 == col, 1.0, 0.0)
+        partf = part.astype(F32)
+        pickb = pick.astype(BF16)
+        pick2 = jnp.concatenate([pickb, pickb], axis=0)
 
         def sample(g, acc):
             s = jnp.dot(
@@ -86,13 +159,14 @@
                 pick2,
                 preferred_element_type=F32,
             )
-            parts = [jnp.zeros((8, 256), F32) for _ in range(4)]
+            parts = [None] * 4
             for k in range(levels):
-                parts[k % 4] = parts[k % 4] + tiles[q, k : k + 1, :] * s[8 * k : 8 * k + 8, :]
-            total = (parts[0] + parts[1]) + (parts[2] + parts[3])
-            return acc + jnp.where(group == g, total, 0.0)
-
-        acc = lax.fori_loop(gmin, gmax + 1, sample, jnp.zeros((8, 256), F32))
+                x = tiles[q, k : k + 1, at_r] * s[8 * k : 8 * k + 8, :]
+                parts[k % 4] = x if parts[k % 4] is None else parts[k % 4] + x
+            total_g = (parts[0] + parts[1]) + (parts[2] + parts[3])
+            return acc + jnp.where(group == g, total_g, 0.0)
+
+        acc = lax.fori_loop(gmin, gmax + 1, sample, jnp.zeros((8, wide), F32))
         equiv = jnp.sum(jnp.where(rmask, acc, 0.0), axis=0, keepdims=True)
         scaled = (value - equiv) * inverse
         magnitude = jnp.abs(scaled)
@@ -102,20 +176,20 @@
             HUBER_EDGE * magnitude - 0.5 * HUBER_EDGE * HUBER_EDGE,
         )
         response = HUBER_EDGE / jnp.maximum(magnitude, HUBER_EDGE) * scaled * inverse
-        wr = tiles[q, 0:levels, :] * response
+        wr = tiles[q, 0:levels, at_r] * response
         hi = wr.astype(BF16).astype(F32)
         whi[0:levels, :] = hi
         wlo[0:levels, :] = wr - hi
-        iota256 = lax.broadcasted_iota(jnp.int32, (256, 256), 0)
-        place = jnp.where(iota256 == col + 128 * part, 1.0, 0.0).astype(BF16)
+        low = pick * partf
+        place = jnp.concatenate([(pick - low).astype(BF16), low.astype(BF16)], axis=0)
         place2 = jnp.concatenate([place, place], axis=1)
 
         def spread(b, _):
             m = jnp.where(rmask & (block == b), 1.0, 0.0)
             for k in range(0, levels, 2):
-                for half, src in ((0, whi), (256, wlo)):
+                for half, src in ((0, whi), (wide, wlo)):
                     x = jnp.concatenate([m * src[k : k + 1, :], m * src[k + 1 : k + 2, :]], axis=0)
-                    amat[8 * k : 8 * k + 16, half : half + 256] = x.astype(BF16)
+                    amat[8 * k : 8 * k + 16, half : half + wide] = x.astype(BF16)
             at = pl.ds(pl.multiple_of(b * rows_in, 8), rows_in)
             force[at, :] += lax.dot_general(
                 amat[...], place2, (((1,), (1,)), ((), ())), preferred_element_type=F32
@@ -125,21 +199,42 @@
         lax.fori_loop(gmin >> 1, (gmax >> 1) + 1, spread, 0)
         return 0
 
-    lax.fori_loop(0, 8, tile, 0)
-
-    @pl.when(step == steps - 1)
-    def _():
-        for b in range(4):
-            for part in range(2):
-                r0 = 32 * part + 8 * b
-                sea = sea_ref[r0 : r0 + 8, :].astype(F32)
-
-                def body(k, _):
-                    f = force[pl.ds(pl.multiple_of(b * rows_in + 8 * k, 8), 8), 128 * part : 128 * part + 128]
-                    state_ref[k, r0 : r0 + 8, :] = sea * es_ref[k, r0 : r0 + 8, :] * f
-                    return 0
-
-                lax.fori_loop(0, levels, body, 0, unroll=5)
+    lax.fori_loop(0, 8 * (total // wide), tile, 0)
+
+    for b in range(4):
+        for part in range(2):
+            r0 = 32 * part + 8 * b
+            sea = sea_ref[r0 : r0 + 8, :].astype(F32)
+
+            def body(k, _):
+                f = force[pl.ds(pl.multiple_of(b * rows_in + 8 * k, 8), 8), 128 * part : 128 * part + 128]
+                state_ref[k, r0 : r0 + 8, :] = sea * es_ref[k, r0 : r0 + 8, :] * f
+                return 0
+
+            lax.fori_loop(0, levels, body, 0, unroll=5)
+
+
+def observe_call(received, bgm, sea_mask, es, wide=WIDE):
+    levels, ny, nx = es.shape
+    owners = received.shape[0] // 56
+    return pl.pallas_call(
+        observe,
+        out_shape=(
+            jax.ShapeDtypeStruct((levels, ny, nx), F32),
+            jax.ShapeDtypeStruct((1, wide), F32),
+        ),
+        in_specs=[vmem(), vmem(), vmem(), vmem()],
+        out_specs=(vmem(), vmem()),
+        scratch_shapes=[
+            pltpu.VMEM((8, 56, 16 * owners), F32),
+            pltpu.VMEM((32 * levels, 256), F32),
+            pltpu.VMEM((56, wide), F32),
+            pltpu.VMEM((56, wide), F32),
+            pltpu.VMEM((8 * levels, 2 * wide), BF16),
+        ],
+        compiler_params=params(),
+        name="observe",
+    )(received, bgm, sea_mask, es)
 
 
 def edges(x_ref, east_ref, west_ref):
@@ -360,17 +455,8 @@
     n_lon = lax.axis_size("lon")
     lat_at = lax.axis_index("lat").astype(jnp.int32)
 
-    slot_index = lax.broadcasted_iota(jnp.int32, (owners, capacity), 1)
-    valid_slot = slot_index < obs_count[0][:, None]
-    inverse = jnp.where(valid_slot, 1.0 / obs_error[0], 0.0)
-    packed = jnp.concatenate(
-        [
-            obs_weight[0],
-            obs_value[0][:, None, :],
-            inverse[:, None, :],
-            obs_column[0].astype(F32)[:, None, :],
-        ],
-        axis=1,
+    packed = pack_call(
+        obs_count, jnp.swapaxes(obs_weight[0], 0, 1), obs_value[0], obs_error[0], obs_column[0]
     )
     received = lax.all_to_all(packed, ("lat", "lon"), split_axis=0, concat_axis=0, tiled=True)
 
@@ -384,7 +470,7 @@
     es = error_scale.reshape(levels, ny, nx)
     bgm = pl.pallas_call(
         split_background,
-        out_shape=jax.ShapeDtypeStruct((8 * levels * 8, 256), BF16),
+        out_shape=jax.ShapeDtypeStruct((64 * levels, 256), BF16),
         in_specs=[vmem()],
         out_specs=vmem(),
         compiler_params=params(),
@@ -392,34 +478,8 @@
         name="split_background",
     )(bg)
 
-    per = 16
-    state, cost = pl.pallas_call(
-        observe,
-        grid=(owners // per,),
-        out_shape=(
-            jax.ShapeDtypeStruct((levels, ny, nx), F32),
-            jax.ShapeDtypeStruct((1, 256), F32),
-        ),
-        in_specs=[
-            pl.BlockSpec((per, levels + 3, capacity), lambda i: (i, 0, 0)),
-            pl.BlockSpec((64 * levels, 256), lambda i: (0, 0)),
-            pl.BlockSpec((ny, nx), lambda i: (0, 0)),
-            pl.BlockSpec((levels, ny, nx), lambda i: (0, 0, 0)),
-        ],
-        out_specs=(
-            pl.BlockSpec((levels, ny, nx), lambda i: (0, 0, 0)),
-            pl.BlockSpec((1, 256), lambda i: (0, 0)),
-        ),
-        scratch_shapes=[
-            pltpu.VMEM((8, 56, 256), F32),
-            pltpu.VMEM((32 * levels, 256), F32),
-            pltpu.VMEM((56, 256), F32),
-            pltpu.VMEM((56, 256), F32),
-            pltpu.VMEM((8 * levels, 512), BF16),
-        ],
-        compiler_params=params(),
-        name="observe",
-    )(received, bgm, sea_mask, es)
+    bgm, cside, cone, ctwo, received = lax.optimization_barrier((bgm, cside, cone, ctwo, received))
+    state, cost = observe_call(received, bgm, sea_mask, es)
 
     share = jnp.sum(cost)
     shares = lax.all_to_all(

time: 381 us -> 238 us (0.62)
  Pallas kernels: 269 us -> 125 us
  blocking collectives: 0 us -> 18.3 us
  starting transfers between devices: 39.1 us -> 32 us
  local copies, waits for them, and re-layouts: 9.53 us -> 5.12 us
    pallas_call x2 -> x3, Pallas kernels: 224 us -> 79.9 us  [the longest x1 67.7 us: observe_call(): pl.pallas_call(observe, out_shape=(jax.ShapeDtypeStruct((levels, ny, nx),...]
    all_to_all x1, waiting for transfers between devices: 39.7 us -> 0.01 us  [shards(): lax.all_to_all(packed, ('lat', 'lon'), split_axis=0, concat_axis=0, tiled...]
    ppermute x2, waiting for transfers between devices: 1.59 us -> 38.6 us  [exchange(): lax.ppermute(to_east, 'lon', [(i, (i + 1) % n_lon) for i in range(n_lon)])]
    all_to_all x0 -> x1, blocking collectives: none -> 18.3 us  [shards(): lax.all_to_all(jnp.broadcast_to(share, (owners, 1, 128)), ('lat', 'lon'),...]
    all_to_all x1 -> x0, starting transfers between devices: 8.6 us -> none  [shards(): lax.all_to_all(jnp.broadcast_to(share, (owners, 1, 128)), ('lat', 'lon'),...]
    unnamed x27 -> x20, local copies, waits for them, and re-layouts: 7.12 us -> 3.25 us
  transfers between devices with their start and end apart: 10 -> 9, of which waited for: 4 -> 4; matrix products, arithmetic and copies ran while one was open for 2% -> 2% of each run, Pallas kernels for 5% -> 3%
where the time goes in v2:
time: 238 us; the launch traced here: 237 us
  Pallas kernels  125 us (53%)
  waiting for transfers between devices  50.7 us (21%)
  starting transfers between devices  32 us (13%)
  blocking collectives  18.3 us (8%)
  local copies, waits for them, and re-layouts  5.12 us (2%)
  between operations  3.2 us (1%)
  other arithmetic  2.59 us (1%)
    pallas_call x1, Pallas kernels, observe_call(): pl.pallas_call(observe, out_shape=(jax.ShapeDtypeStruct((levels, ny, nx),...  67.7 us
    ppermute x2, waiting for transfers between devices, exchange(): lax.ppermute(to_east, 'lon', [(i, (i + 1) % n_lon) for i in range(n_lon)])  38.6 us
    pallas_call x1, Pallas kernels, shards(): pl.pallas_call(diffuse, grid=(levels // blk,), out_shape=jax.ShapeDtypeSt...  22.8 us
    all_to_all x1, blocking collectives, shards(): lax.all_to_all(jnp.broadcast_to(share, (owners, 1, 128)), ('lat', 'lon'),...  18.3 us
    pallas_call x2, Pallas kernels, exchange(): pl.pallas_call(assemble, out_shape=(jax.ShapeDtypeStruct(x.shape, F32), r...  12.9 us
    ppermute x2, waiting for transfers between devices, branch(): lax.ppermute(v, ('lat', 'lon'), perm_of(n_lat, n_lon, rule))  12.1 us
    all_to_all x1, starting transfers between devices, shards(): lax.all_to_all(packed, ('lat', 'lon'), split_axis=0, concat_axis=0, tiled...  10.9 us
    ppermute x2, starting transfers between devices, exchange(): lax.ppermute(to_west, 'lon', [((i + 1) % n_lon, i) for i in range(n_lon)])  10.7 us
  transfers between devices with their start and end apart: 9, of which 4 were waited for; matrix products, arithmetic and copies ran while one was open for 2% of the time, Pallas kernels for 3%

profile of v2, /device:TPU:6, one launch (start us, length us, event | category | flops | bytes accessed | tf_op | source)
XLA Modules:
  0.0 236.7 jit_solution(14942324302074740563)
XLA Ops:
  0.6 9.1 %pack.1 = f32[7168,128]{1,0:T(8,128)} custom-call(s32[1,128]{1,0:T(1,128)} %count_ref.1, f32[50,128,128]{2,1,0:T(8,128)} %bitcast.23, f32[128,128]{1,0:T(8,128)} %bitcast.26, f32[128,128]{1,0:T(8,128)} %bitcast.27, s32[128,128]{1,0:T(8,128)} %bitcast.28), custom_call_target="tpu_custom_call" | custom-call | tf_op jit(solution)/shard_map/pack/pallas_call | solution.py:86
  9.8 10.9 %all-to-all-start = ((f32[128,56,128]{2,1,0:T(8,128)}), f32[128,56,128]{2,1,0:T(8,128)}, u32[]{:S(2)}, u32[]{:S(2)}) async-start(f32[128,56,128]{2,1,0:T(8,128)} %bitcast.20), calls=%async_computation | async-start | bytes 7340032 | tf_op jit(solution)/shard_map/all_to_all | solution.py:461
  21.3 1.8 edges.2
  23.3 5.3 %collective-permute-start.33 = (f32[3,8,128]{2,1,0:T(8,128)}, f32[3,8,128]{2,1,0:T(8,128)S(1)}, u32[]{:S(2)}, u32[]{:S(2)}) collective-permute-start(f32[3,8,128]{2,1,0:T(8,128)} %get-tuple-element.86), channel_id=1, source_target_pairs={{1,0},{2,1},{3,2},{4,3},{5,4},{6,5},{7,6},{8,7},{9,8},{10,9},{11,1... | collective-permute-start | bytes 36872 | tf_op jit(solution)/shard_map/ppermute | solution.py:409
  28.6 1.2 slice.6
  31.1 34.9 %collective-permute-done.32.fw_ref = f32[3,8,128]{2,1,0:T(8,128)S(1)} collective-permute-done((f32[3,8,128]{2,1,0:T(8,128)}, f32[3,8,128]{2,1,0:T(8,128)S(1)}, u32[]{:S(2)}, u32[]{:S(2)}) %collective-permute-start.32) | collective-permute-done | bytes 12320 | tf_op jit(solution)/shard_map/ppermute | solution.py:408
  67.2 2.1 assemble.2
  69.3 1.4 collective-permute-start.34
  70.8 3.1 %split_background.1.bgm_ref = bf16[3200,256]{1,0:T(8,128)(2,1)} custom-call(f32[50,64,128]{2,1,0:T(8,128)} %bitcast.24), custom_call_target="tpu_custom_call" | custom-call | flops 3000000 | bytes 3300000 | tf_op jit(solution)/shard_map/split_background/pallas_call | solution.py:471
  73.9 7.8 %conditional.2 = (f32[3,4,256]{2,1,0:T(4,128)}) conditional(s32[]{:T(128)} %clamp.4, f32[3,4,256]{2,1,0:T(4,128)S(1)} %get-tuple-element.89, f32[3,4,256]{2,1,0:T(4,128)S(1)} %get-tuple-element.89, f32[3,4,256]{2,1,0:T(4,128)S(1)} %get-tuple-element.89, f32[3,4,256]{2,1,0:T(4,128)S(1)} %get-tuple-element.89, ...), branch_computations={%region_0.1_spmd, %region_1.2_spmd, %region_2.3_spmd, %region_3.4_... | conditional | bytes 49200 | solution.py:432
  73.9 4.5 %collective-permute-start.14 = (f32[3,4,256]{2,1,0:T(4,128)S(1)}, f32[3,4,256]{2,1,0:T(4,128)}, u32[]{:S(2)}, u32[]{:S(2)}) collective-permute-start(f32[3,4,256]{2,1,0:T(4,128)S(1)} %param.14), channel_id=1, source_target_pairs={{16,32},{17,33},{18,34},{19,35},{20,36},{21,37},{22,38},{23,39},{2... | collective-permute-start | bytes 36872 | tf_op jit(solution)/shard_map/cond/branch_14_fun/ppermute | solution.py:430
  78.4 3.2 %collective-permute-done.14 = f32[3,4,256]{2,1,0:T(4,128)} collective-permute-done((f32[3,4,256]{2,1,0:T(4,128)S(1)}, f32[3,4,256]{2,1,0:T(4,128)}, u32[]{:S(2)}, u32[]{:S(2)}) %collective-permute-start.14) | collective-permute-done | bytes 12320 | tf_op jit(solution)/shard_map/cond/branch_14_fun/ppermute | solution.py:430
  81.7 67.7 %observe.1 = (f32[50,64,128]{2,1,0:T(8,128)}, f32[1,2048]{1,0:T(1,128)}) custom-call(f32[7168,128]{1,0:T(8,128)} %bitcast.15.rec_ref, bf16[3200,256]{1,0:T(8,128)(2,1)} %split_background.1.bgm_ref, s32[64,128]{1,0:T(8,128)} %sea_ref.1, f32[50,64,128]{2,1,0:T(8,128)} %bitcast.21), custom_call_target="tpu_custom_call" | custom-call | tf_op jit(solution)/shard_map/observe/pallas_call | solution.py:220
  149.4 7.3 %edges.3 = (f32[50,8,128]{2,1,0:T(8,128)}, f32[50,8,128]{2,1,0:T(8,128)}) custom-call(f32[50,64,128]{2,1,0:T(8,128)} %get-tuple-element.92.x_ref), custom_call_target="tpu_custom_call" | custom-call | flops 50000 | bytes 2000000 | tf_op jit(solution)/shard_map/edges/pallas_call | solution.py:399
  156.6 5.4 %collective-permute-start.36 = (f32[50,8,128]{2,1,0:T(8,128)}, f32[50,8,128]{2,1,0:T(8,128)S(1)}, u32[]{:S(2)}, u32[]{:S(2)}) collective-permute-start(f32[50,8,128]{2,1,0:T(8,128)} %get-tuple-element.94), channel_id=1, source_target_pairs={{1,0},{2,1},{3,2},{4,3},{5,4},{6,5},{7,6},{8,7},{9,8},{10,9},{11,1... | collective-permute-start | bytes 614408 | tf_op jit(solution)/shard_map/ppermute | solution.py:409
  162.0 3.6 %collective-permute-done.35.fw_ref = f32[50,8,128]{2,1,0:T(8,128)S(1)} collective-permute-done((f32[50,8,128]{2,1,0:T(8,128)}, f32[50,8,128]{2,1,0:T(8,128)S(1)}, u32[]{:S(2)}, u32[]{:S(2)}) %collective-permute-start.35) | collective-permute-done | bytes 204832 | tf_op jit(solution)/shard_map/ppermute | solution.py:408
  166.3 0.7 copy-done.1
  167.0 10.8 %assemble.3 = (f32[50,64,128]{2,1,0:T(8,128)}, f32[50,4,256]{2,1,0:T(4,128)}, f32[50,4,256]{2,1,0:T(4,128)S(1)}) custom-call(s32[4]{0:T(128)} %pad_add_fusion.info_ref, f32[50,64,128]{2,1,0:T(8,128)} %get-tuple-element.92.x_ref, f32[50,8,128]{2,1,0:T(8,128)} %copy-done, f32[50,8,128]{2,1,0:T(8,128)} %copy-done.1), custom_call_target="tpu_custom_call" | custom-call | flops 50000 | bytes 4000000 | tf_op jit(solution)/shard_map/assemble/pallas_call | solution.py:411
  179.1 18.3 %all_to_all.17 = f32[128,1,128]{2,1,0:T(1,128)S(1)} all-to-all(f32[128,1,128]{2,1,0:T(1,128)S(1)} %broadcast_in_dim.3), channel_id=1, replica_groups=mesh['lat'=8,'lon'=16] {'lat','lon'}, dimensions={0} | all-to-all | bytes 131072 | tf_op jit(solution)/shard_map/all_to_all | solution.py:485
  197.5 0.7 slice_reduce_fusion
  198.8 13.2 %conditional.3 = (f32[50,4,256]{2,1,0:T(4,128)}) conditional(s32[]{:T(128)} %clamp.4, f32[50,4,256]{2,1,0:T(4,128)S(1)} %get-tuple-element.97, f32[50,4,256]{2,1,0:T(4,128)S(1)} %get-tuple-element.97, f32[50,4,256]{2,1,0:T(4,128)S(1)} %get-tuple-element.97, f32[50,4,256]{2,1,0:T(4,128)S(1)} %get-tuple-element.97, ...), branch_computations={%region_16.17_spmd, %region_17.18_spmd, %region_18.19_spmd, %regio... | conditional | bytes 819248 | solution.py:432
  198.9 4.3 %collective-permute-start.30 = (f32[50,4,256]{2,1,0:T(4,128)S(1)}, f32[50,4,256]{2,1,0:T(4,128)}, u32[]{:S(2)}, u32[]{:S(2)}) collective-permute-start(f32[50,4,256]{2,1,0:T(4,128)S(1)} %param.30), channel_id=1, source_target_pairs={{16,32},{17,33},{18,34},{19,35},{20,36},{21,37},{22,38},{23,39},{2... | collective-permute-start | bytes 614408 | tf_op jit(solution)/shard_map/cond/branch_14_fun/ppermute | solution.py:430
  203.2 8.9 %collective-permute-done.30 = f32[50,4,256]{2,1,0:T(4,128)} collective-permute-done((f32[50,4,256]{2,1,0:T(4,128)S(1)}, f32[50,4,256]{2,1,0:T(4,128)}, u32[]{:S(2)}, u32[]{:S(2)}) %collective-permute-start.30) | collective-permute-done | bytes 204832 | tf_op jit(solution)/shard_map/cond/branch_14_fun/ppermute | solution.py:430
  212.7 22.8 %diffuse.1 = f32[50,64,128]{2,1,0:T(8,128)} custom-call(s32[4]{0:T(128)} %pad_add_fusion.info_ref, f32[50,64,128]{2,1,0:T(8,128)} %get-tuple-element.92.x_ref, f32[50,64,128]{2,1,0:T(8,128)} %get-tuple-element.95.side_ref, f32[50,4,256]{2,1,0:T(4,128)} %copy-done.2, f32[50,4,256]{2,1,0:T(4,128)} %get-tuple-element.103.two_ref, ...), custom_call_target="tpu_custom_call" | custom-call | tf_op jit(solution)/shard_map/diffuse/pallas_call | solution.py:495
  (32 shorter events, 5.3 us)
Async XLA Ops:
  9.8 10.9 %copy-start.3 = (s32[64,128]{1,0:T(8,128)S(1)}, s32[64,128]{1,0:T(8,128)}, u32[]{:S(2)}) copy-start(s32[64,128]{1,0:T(8,128)} %sea_ref.1) | copy-start | bytes 98308
  9.8 10.9 %copy-start.4 = (f32[64,128]{1,0:T(8,128)S(1)}, f32[64,128]{1,0:T(8,128)}, u32[]{:S(2)}) copy-start(f32[64,128]{1,0:T(8,128)} %param.46) | copy-start | bytes 98308
  9.8 10.9 %copy-start.5 = (f32[64,128]{1,0:T(8,128)S(1)}, f32[64,128]{1,0:T(8,128)}, u32[]{:S(2)}) copy-start(f32[64,128]{1,0:T(8,128)} %param.45) | copy-start | bytes 98308
  9.8 71.9 %all-to-all-start = ((f32[128,56,128]{2,1,0:T(8,128)}), f32[128,56,128]{2,1,0:T(8,128)}, u32[]{:S(2)}, u32[]{:S(2)}) async-start(f32[128,56,128]{2,1,0:T(8,128)} %bitcast.20), calls=%async_computation | async-start | bytes 7340032 | tf_op jit(solution)/shard_map/all_to_all | solution.py:461
  23.1 42.9 %collective-permute-start.32 = (f32[3,8,128]{2,1,0:T(8,128)}, f32[3,8,128]{2,1,0:T(8,128)S(1)}, u32[]{:S(2)}, u32[]{:S(2)}) collective-permute-start(f32[3,8,128]{2,1,0:T(8,128)} %get-tuple-element.85), channel_id=1, source_target_pairs={{0,1},{1,2},{2,3},{3,4},{4,5},{5,6},{6,7},{7,8},{8,9},{9,10},{10,1... | collective-permute-start | bytes 36872 | tf_op jit(solution)/shard_map/ppermute | solution.py:408
  23.3 42.8 %collective-permute-start.33 = (f32[3,8,128]{2,1,0:T(8,128)}, f32[3,8,128]{2,1,0:T(8,128)S(1)}, u32[]{:S(2)}, u32[]{:S(2)}) collective-permute-start(f32[3,8,128]{2,1,0:T(8,128)} %get-tuple-element.86), channel_id=1, source_target_pairs={{1,0},{2,1},{3,2},{4,3},{5,4},{6,5},{7,6},{8,7},{9,8},{10,9},{11,1... | collective-permute-start | bytes 36872 | tf_op jit(solution)/shard_map/ppermute | solution.py:409
  66.1 0.6 copy-start.7
  66.7 0.6 copy-start.8
  69.3 12.3 %collective-permute-start.34 = (f32[3,4,256]{2,1,0:T(4,128)}, f32[3,4,256]{2,1,0:T(4,128)S(1)}, u32[]{:S(2)}, u32[]{:S(2)}) collective-permute-start(f32[3,4,256]{2,1,0:T(4,128)} %get-tuple-element.88), channel_id=1, source_target_pairs={{0,16},{1,17},{2,18},{3,19},{4,20},{5,21},{6,22},{7,23},{8,24},{9,... | collective-permute-start | bytes 36872 | tf_op jit(solution)/shard_map/ppermute | solution.py:420
  73.9 7.8 %collective-permute-start.14 = (f32[3,4,256]{2,1,0:T(4,128)S(1)}, f32[3,4,256]{2,1,0:T(4,128)}, u32[]{:S(2)}, u32[]{:S(2)}) collective-permute-start(f32[3,4,256]{2,1,0:T(4,128)S(1)} %param.14), channel_id=1, source_target_pairs={{16,32},{17,33},{18,34},{19,35},{20,36},{21,37},{22,38},{23,39},{2... | collective-permute-start | bytes 36872 | tf_op jit(solution)/shard_map/cond/branch_14_fun/ppermute | solution.py:430
  81.7 67.7 %copy-start.6 = (f32[3,4,256]{2,1,0:T(4,128)}, f32[3,4,256]{2,1,0:T(4,128)S(1)}, u32[]{:S(2)}) copy-start(f32[3,4,256]{2,1,0:T(4,128)S(1)} %collective-permute-done.34.cone_ref) | copy-start | bytes 36868
  149.4 28.4 %copy-start.9 = (f32[1,2048]{1,0:T(1,128)S(1)}, f32[1,2048]{1,0:T(1,128)}, u32[]{:S(2)}) copy-start(f32[1,2048]{1,0:T(1,128)} %get-tuple-element.101) | copy-start | bytes 24580
  156.6 9.0 %collective-permute-start.35 = (f32[50,8,128]{2,1,0:T(8,128)}, f32[50,8,128]{2,1,0:T(8,128)S(1)}, u32[]{:S(2)}, u32[]{:S(2)}) collective-permute-start(f32[50,8,128]{2,1,0:T(8,128)} %get-tuple-element.93), channel_id=1, source_target_pairs={{0,1},{1,2},{2,3},{3,4},{4,5},{5,6},{6,7},{7,8},{8,9},{9,10},{10,1... | collective-permute-start | bytes 614408 | tf_op jit(solution)/shard_map/ppermute | solution.py:408
  156.6 9.0 %collective-permute-start.36 = (f32[50,8,128]{2,1,0:T(8,128)}, f32[50,8,128]{2,1,0:T(8,128)S(1)}, u32[]{:S(2)}, u32[]{:S(2)}) collective-permute-start(f32[50,8,128]{2,1,0:T(8,128)} %get-tuple-element.94), channel_id=1, source_target_pairs={{1,0},{2,1},{3,2},{4,3},{5,4},{6,5},{7,6},{8,7},{9,8},{10,9},{11,1... | collective-permute-start | bytes 614408 | tf_op jit(solution)/shard_map/ppermute | solution.py:409
  165.6 0.7 copy-start
  166.3 0.7 copy-start.1
  177.8 34.2 %collective-permute-start.37 = (f32[50,4,256]{2,1,0:T(4,128)}, f32[50,4,256]{2,1,0:T(4,128)S(1)}, u32[]{:S(2)}, u32[]{:S(2)}) collective-permute-start(f32[50,4,256]{2,1,0:T(4,128)} %get-tuple-element.96), channel_id=1, source_target_pairs={{0,16},{1,17},{2,18},{3,19},{4,20},{5,21},{6,22},{7,23},{8,24},{9,... | collective-permute-start | bytes 614408 | tf_op jit(solution)/shard_map/ppermute | solution.py:420
  198.9 13.2 %collective-permute-start.30 = (f32[50,4,256]{2,1,0:T(4,128)S(1)}, f32[50,4,256]{2,1,0:T(4,128)}, u32[]{:S(2)}, u32[]{:S(2)}) collective-permute-start(f32[50,4,256]{2,1,0:T(4,128)S(1)} %param.30), channel_id=1, source_target_pairs={{16,32},{17,33},{18,34},{19,35},{20,36},{21,37},{22,38},{23,39},{2... | collective-permute-start | bytes 614408 | tf_op jit(solution)/shard_map/cond/branch_14_fun/ppermute | solution.py:430
  212.1 0.7 copy-start.2

commit v3 on v2

v3 whole, which is shorter than its diff:
```python
import jax
import jax.numpy as jnp
from jax import lax
from jax.experimental import pallas as pl
from jax.experimental.pallas import tpu as pltpu
from jax.sharding import PartitionSpec as P

STEPS = 4
HALO = 4
HUBER_EDGE = 1.5
F32 = jnp.float32
BF16 = jnp.bfloat16
WIDE = 2048
DEEP = 56
UNROLL_DIFFUSE = 4
VMEM_LIMIT = 56 * 1024 * 1024


def split_background(bg_ref, out_ref):
    levels = bg_ref.shape[0]
    for h in range(4):
        for p in range(2):
            base = (2 * h + p) * levels * 8
            row = 32 * p + 8 * h

            def body(i, _):
                a = bg_ref[2 * i, row : row + 8, :]
                b = bg_ref[2 * i + 1, row : row + 8, :]
                x = jnp.concatenate([a, b], axis=0)
                hi = x.astype(BF16)
                lo = (x - hi.astype(F32)).astype(BF16)
                at = pl.ds(pl.multiple_of(base + i * 16, 16), 16)
                out_ref[at, 0:128] = hi
                out_ref[at, 128:256] = lo
                return 0

            lax.fori_loop(0, levels // 2, body, 0, unroll=5)


def pack(count_ref, w_ref, value_ref, error_ref, cell_ref, out_ref, order_ref, counts_ref):
    levels, some, n = w_ref.shape
    owners = order_ref.shape[0]
    lane8 = lax.broadcasted_iota(jnp.int32, (8, n), 1)

    @pl.when(pl.program_id(0) == 0)
    def _():
        counts = jnp.transpose(jnp.broadcast_to(count_ref[...].astype(F32), (owners, n)))
        lane = lax.broadcasted_iota(jnp.int32, (owners, n), 1)
        cell = cell_ref[...]
        row = cell >> 7
        key = (((row >> 3) & 3) << 11) | ((row >> 5) << 10) | ((row & 7) << 7) | (cell & 127)
        counts_ref[...] = counts.astype(jnp.int32)
        filled = lane.astype(F32) < counts
        spread = (lane.astype(F32) - counts + 0.5) * (8192.0 / jnp.maximum(n - counts, 1.0))
        key = jnp.where(filled, key, jnp.clip(spread, 0.0, 8191.0).astype(jnp.int32))
        x = (key * n + lane).astype(F32)
        size = 2
        while size <= n:
            step = size // 2
            while step >= 1:
                first = (lane & step) == 0
                other = jnp.where(first, pltpu.roll(x, n - step, axis=1), pltpu.roll(x, step, axis=1))
                least = first == ((lane & size) == 0)
                x = jnp.where(least, jnp.minimum(x, other), jnp.maximum(x, other))
                step //= 2
            size *= 2
        order_ref[...] = x.astype(jnp.int32) & (n - 1)

    for o in range(0, some, 8):
        at = pl.ds(pl.multiple_of(pl.program_id(0) * some + o, 8), 8)
        order = order_ref[at, :]
        valid = order < counts_ref[at, :]

        def put(k, v):
            out_ref[pl.ds(o * 56 + k, 8, stride=56), :] = v

        for k in range(levels):
            put(k, jnp.take_along_axis(w_ref[k, o : o + 8, :], order, axis=1))
        put(levels, jnp.take_along_axis(value_ref[at, :], order, axis=1))
        error = jnp.take_along_axis(error_ref[at, :], order, axis=1)
        put(levels + 1, jnp.where(valid, 1.0 / error, 0.0))
        put(levels + 2, jnp.take_along_axis(cell_ref[at, :], order, axis=1).astype(F32))
        for k in range(levels + 3, 56):
            put(k, jnp.zeros((8, n), F32))


def pack_call(count, weight, value, error, column):
    levels, owners, n = weight.shape
    some = 16
    return pl.pallas_call(
        pack,
        grid=(owners // some,),
        out_shape=jax.ShapeDtypeStruct((owners * 56, n), F32),
        in_specs=[
            pl.BlockSpec((1, owners), lambda i: (0, 0)),
            pl.BlockSpec((levels, some, n), lambda i: (0, i, 0)),
            pl.BlockSpec((owners, n), lambda i: (0, 0)),
            pl.BlockSpec((owners, n), lambda i: (0, 0)),
            pl.BlockSpec((owners, n), lambda i: (0, 0)),
        ],
        out_specs=pl.BlockSpec((some * 56, n), lambda i: (i, 0)),
        scratch_shapes=[pltpu.VMEM((owners, n), jnp.int32), pltpu.VMEM((owners, n), jnp.int32)],
        compiler_params=params(),
        name="pack",
    )(count, weight, value, error, column)


def observe(rec_ref, bgm_ref, east_ref, north_ref, sea_ref, es_ref, state_ref, to_east_ref, to_west_ref, cost_ref, tiles, force, whi, wlo, amat):
    levels = es_ref.shape[0]
    sources = rec_ref.shape[0] // 56
    rows_in = 8 * levels
    wide = whi.shape[1]
    total = tiles.shape[2]

    force[...] = jnp.zeros_like(force)
    cost_ref[...] = jnp.zeros_like(cost_ref)

    def regroup(eight, _):
        lane = lax.broadcasted_iota(jnp.int32, (8, 128), 1)
        for r in range(0, 56, 8):
            xs = [rec_ref[pl.ds(pl.multiple_of((eight * 8 + i) * 56 + r, 8), 8), :] for i in range(8)]
            for d in (1, 2, 4):
                keep = (lane // (16 * d)) % 2 == 0
                new = list(xs)
                for i in range(8):
                    if i & d == 0:
                        lo, hi = xs[i], xs[i + d]
                        new[i] = jnp.where(keep, lo, pltpu.roll(hi, 16 * d, axis=1))
                        new[i + d] = jnp.where(keep, pltpu.roll(lo, 128 - 16 * d, axis=1), hi)
                xs = new
            for i in range(8):
                tiles[i, r : r + 8, pl.ds(pl.multiple_of(eight * 128, 128), 128)] = xs[i]
        return 0

    lax.fori_loop(0, sources // 8, regroup, 0)

    iota8 = lax.broadcasted_iota(jnp.int32, (8, wide), 0)

    def tile(t, _):
        q = t // (total // wide)
        at_r = pl.ds(pl.multiple_of((t % (total // wide)) * wide, wide), wide)
        value = tiles[q, levels : levels + 1, at_r]
        inverse = tiles[q, levels + 1 : levels + 2, at_r]
        cell = tiles[q, levels + 2 : levels + 3, at_r].astype(jnp.int32)
        row = cell >> 7
        col = cell & 127
        part = row >> 5
        block = (row >> 3) & 3
        group = 2 * block + part
        valid = inverse > 0.0
        gmin = jnp.min(jnp.where(valid, group, 8))
        gmax = jnp.max(jnp.where(valid, group, -1))
        rmask = iota8 == (row & 7)
        iota128 = lax.broadcasted_iota(jnp.int32, (128, wide), 0)
        pick = jnp.where(iota128 == col, 1.0, 0.0)
        partf = part.astype(F32)
        pickb = pick.astype(BF16)
        pick2 = jnp.concatenate([pickb, pickb], axis=0)

        def sample(g, acc):
            s = jnp.dot(
                bgm_ref[pl.ds(pl.multiple_of(g * rows_in, 16), rows_in), :],
                pick2,
                preferred_element_type=F32,
            )
            parts = [None] * 4
            for k in range(levels):
                x = tiles[q, k : k + 1, at_r] * s[8 * k : 8 * k + 8, :]
                parts[k % 4] = x if parts[k % 4] is None else parts[k % 4] + x
            total_g = (parts[0] + parts[1]) + (parts[2] + parts[3])
            return acc + jnp.where(group == g, total_g, 0.0)

        acc = lax.fori_loop(gmin, gmax + 1, sample, jnp.zeros((8, wide), F32))
        equiv = jnp.sum(jnp.where(rmask, acc, 0.0), axis=0, keepdims=True)
        scaled = (value - equiv) * inverse
        magnitude = jnp.abs(scaled)
        cost_ref[...] += jnp.where(
            magnitude <= HUBER_EDGE,
            0.5 * scaled * scaled,
            HUBER_EDGE * magnitude - 0.5 * HUBER_EDGE * HUBER_EDGE,
        )
        response = HUBER_EDGE / jnp.maximum(magnitude, HUBER_EDGE) * scaled * inverse
        wr = tiles[q, 0:levels, at_r] * response
        hi = wr.astype(BF16).astype(F32)
        whi[0:levels, :] = hi
        wlo[0:levels, :] = wr - hi
        low = pick * partf
        place = jnp.concatenate([(pick - low).astype(BF16), low.astype(BF16)], axis=0)
        place2 = jnp.concatenate([place, place], axis=1)

        def spread(b, _):
            m = jnp.where(rmask & (block == b), 1.0, 0.0)
            for k in range(0, levels, 2):
                for half, src in ((0, whi), (wide, wlo)):
                    x = jnp.concatenate([m * src[k : k + 1, :], m * src[k + 1 : k + 2, :]], axis=0)
                    amat[8 * k : 8 * k + 16, half : half + wide] = x.astype(BF16)
            at = pl.ds(pl.multiple_of(b * rows_in, 8), rows_in)
            force[at, :] += lax.dot_general(
                amat[...], place2, (((1,), (1,)), ((), ())), preferred_element_type=F32
            )
            return 0

        lax.fori_loop(gmin >> 1, (gmax >> 1) + 1, spread, 0)
        return 0

    lax.fori_loop(0, 8 * (total // wide), tile, 0)

    for r0 in range(0, 64, 8):
        b, part = (r0 // 8) % 4, r0 // 32
        sea = sea_ref[r0 : r0 + 8, :].astype(F32)

        def level_rows(k):
            return pl.ds(r0 * DEEP + k, 8, stride=DEEP)

        state_ref[level_rows(levels), :] = east_ref[r0 : r0 + 8, :]
        state_ref[level_rows(levels + 1), :] = north_ref[r0 : r0 + 8, :]
        state_ref[level_rows(levels + 2), :] = sea
        for k in range(levels + 3, DEEP):
            state_ref[level_rows(k), :] = jnp.zeros((8, 128), F32)
        for k in range(levels):
            f = force[b * rows_in + 8 * k : b * rows_in + 8 * k + 8, 128 * part : 128 * part + 128]
            state_ref[level_rows(k), :] = sea * es_ref[k, r0 : r0 + 8, :] * f

    lane = lax.broadcasted_iota(jnp.int32, (8, 128), 1)

    def messages(g, _):
        def row(r):
            return state_ref[pl.ds(pl.multiple_of(r * DEEP + 8 * g, 8), 8), :]

        here = pl.ds(pl.multiple_of(8 * g, 8), 8)
        for half in range(2):
            last = jnp.zeros((8, 128), F32)
            first = jnp.zeros((8, 128), F32)
            for i in range(32):
                x = row(32 * half + i)
                mine = (lane >> 2) == i
                last = jnp.where(mine, pltpu.roll(x, (4 * i + 4) % 128, axis=1), last)
                first = jnp.where(mine, pltpu.roll(x, 4 * i, axis=1), first)
            to_east_ref[here, 128 * half : 128 * half + 128] = last
            to_west_ref[here, 128 * half : 128 * half + 128] = first
        more = jnp.zeros((8, 128), F32)
        for d in range(4):
            x = row(60 + d)
            to_east_ref[here, 256 + 128 * d : 384 + 128 * d] = x
            more = jnp.where((lane >> 2) == d, pltpu.roll(x, (4 * d - 4) % 128, axis=1), more)
        to_west_ref[here, 256:384] = more
        return 0

    lax.fori_loop(0, DEEP // 8, messages, 0)


def observe_call(received, bgm, east_rate, north_rate, sea_mask, es, wide=WIDE):
    levels, ny, nx = es.shape
    owners = received.shape[0] // 56
    return pl.pallas_call(
        observe,
        out_shape=(
            jax.ShapeDtypeStruct((ny * DEEP, nx), F32),
            jax.ShapeDtypeStruct((DEEP, 768), F32),
            jax.ShapeDtypeStruct((DEEP, 384), F32),
            jax.ShapeDtypeStruct((1, wide), F32),
        ),
        in_specs=[vmem()] * 6,
        out_specs=(vmem(),) * 4,
        scratch_shapes=[
            pltpu.VMEM((8, 56, 16 * owners), F32),
            pltpu.VMEM((32 * levels, 256), F32),
            pltpu.VMEM((56, wide), F32),
            pltpu.VMEM((56, wide), F32),
            pltpu.VMEM((8 * levels, 2 * wide), BF16),
        ],
        compiler_params=params(),
        name="observe",
    )(received, bgm, east_rate, north_rate, sea_mask, es)


def side_tile(fe, fw, r, lane):
    half, i = r // 32, r % 32
    e = pltpu.roll(fe[128 * half], (128 - 4 * i) % 128, axis=1)
    w = pltpu.roll(fw[128 * half], (124 - 4 * i) % 128, axis=1)
    return jnp.where(lane < 64, e, w)


def assemble(info_ref, bot_ref, top_ref, fw_ref, fe_ref, one_ref, two_ref):
    shift = info_ref[0]
    even = info_ref[1] == 1
    fold = info_ref[2] == 1
    lane = lax.broadcasted_iota(jnp.int32, (8, 128), 1)
    rel_a = shift + 3 - lane
    rel_b = jnp.where(lane < 64, shift + 3 - 128 - lane, shift + 3 + 128 - lane)

    def mirror(west, own, east, rel):
        idx = rel & 127
        w = jnp.take_along_axis(west, idx, axis=1)
        o = jnp.take_along_axis(own, idx, axis=1)
        e = jnp.take_along_axis(east, idx, axis=1)
        return jnp.where(rel < 0, w, jnp.where(rel < 128, o, e))

    def body(g, _):
        here = pl.ds(pl.multiple_of(8 * g, 8), 8)
        fe = {c: fe_ref[here, c : c + 128] for c in (0, 128, 256)}
        fw = {c: fw_ref[here, c : c + 128] for c in range(0, 768, 128)}
        top = [top_ref[d, here, :] for d in range(4)]
        top_side = [side_tile(fe, fw, 60 + d, lane) for d in range(4)]
        for d in range(4):
            u = 3 - d
            east = jnp.where(lane < 4, top_side[u], pltpu.roll(fe[256], (4 - 4 * u) % 128, axis=1))
            fold_a = mirror(fw[256 + 128 * u], top[u], east, rel_a)
            fold_b = mirror(fw[256 + 128 * u], top[u], east, rel_b)
            bot = bot_ref[d, here, :]
            bot_side = side_tile(fe, fw, d, lane)
            one_ref[d, here, 0:128] = jnp.where(even, top[d], bot)
            one_ref[d, here, 128:256] = jnp.where(even, top_side[d], bot_side)
            two_ref[d, here, 0:128] = jnp.where(even, bot, jnp.where(fold, fold_a, top[d]))
            two_ref[d, here, 128:256] = jnp.where(even, bot_side, jnp.where(fold, fold_b, top_side[d]))
        return 0

    lax.fori_loop(0, DEEP // 8, body, 0)


def diffuse(info_ref, x_ref, fw_ref, fe_ref, one_ref, two_ref, es_ref, out_ref, sa, sb, coef):
    levels = es_ref.shape[0] // 64
    even = info_ref[1] == 1
    lane = lax.broadcasted_iota(jnp.int32, (8, 128), 1)

    def fill(g, _):
        here = pl.ds(pl.multiple_of(8 * g, 8), 8)
        fe = {c: fe_ref[here, c : c + 128] for c in (0, 128)}
        fw = {c: fw_ref[here, c : c + 128] for c in (0, 128)}
        for r in range(64):
            sa[r + 4, here, 0:128] = x_ref[r, here, :]
            sa[r + 4, here, 128:256] = side_tile(fe, fw, r, lane)
        for d in range(4):
            one = one_ref[d, here, :]
            two = two_ref[d, here, :]
            sa[d, here, :] = jnp.where(even, two, one)
            sa[68 + d, here, :] = jnp.where(even, one, two)
        return 0

    lax.fori_loop(0, DEEP // 8, fill, 0)

    rows, cols = sa.shape[0], sa.shape[2]
    col = lax.broadcasted_iota(jnp.int32, (rows, cols), 1)
    live = (col < 132) | (col >= 252)
    sea = jnp.where(live, sa[:, levels + 2, :], 0.0)
    east = jnp.where(live, sa[:, levels, :], 0.0) * sea
    north = jnp.where(live, sa[:, levels + 1, :], 0.0) * sea
    a_e = east * pltpu.roll(sea, cols - 1, axis=1)
    a_w = east * pltpu.roll(sea, 1, axis=1)
    a_n = north * pltpu.roll(sea, rows - 1, axis=0)
    a_s = north * pltpu.roll(sea, 1, axis=0)
    coef[0] = 1.0 - ((a_e + a_w) + (a_n + a_s))
    coef[1] = a_e
    coef[2] = a_w
    coef[3] = a_n
    coef[4] = a_s

    def step(src, lo, hi, put):
        def body(r, _):
            c = [coef[i, pl.ds(r, 1), :] for i in range(5)]
            for g in range(DEEP // 8):
                here = slice(8 * g, 8 * g + 8)
                s = src[r, here, :]
                put(
                    r,
                    g,
                    c[0] * s
                    + (c[1] * pltpu.roll(s, cols - 1, axis=1) + c[2] * pltpu.roll(s, 1, axis=1))
                    + (c[3] * src[r + 1, here, :] + c[4] * src[r - 1, here, :]),
                )
            return 0

        lax.fori_loop(lo, hi, body, 0, unroll=UNROLL_DIFFUSE)

    def keep(dst):
        def put(r, g, v):
            dst[r, 8 * g : 8 * g + 8, :] = v

        return put

    def finish(r, g, v):
        n = min(8, levels - 8 * g)
        at = pl.ds(8 * g * 64 + r - 4, n, stride=64)
        out_ref[at, :] = es_ref[at, :] * v[0:n, 0:128]

    step(sa, 1, 71, keep(sb))
    step(sb, 2, 70, keep(sa))
    step(sa, 3, 69, keep(sb))
    step(sb, 4, 68, finish)


def vmem():
    return pl.BlockSpec(memory_space=pltpu.VMEM)


def smem():
    return pl.BlockSpec(memory_space=pltpu.SMEM)


def params():
    return pltpu.CompilerParams(vmem_limit_bytes=VMEM_LIMIT)


def perm_of(n_lat, n_lon, rule):
    pairs = []
    for a in range(n_lat):
        for b in range(n_lon):
            to = rule(a, b)
            if to is not None:
                pairs.append((a * n_lon + b, to[0] * n_lon + to[1] % n_lon))
    return pairs


def assemble_call(info, state, from_west, from_east):
    rows = jax.ShapeDtypeStruct((4, DEEP, 256), F32)
    return pl.pallas_call(
        assemble,
        grid=(1,),
        out_shape=(rows, rows),
        in_specs=[
            smem(),
            pl.BlockSpec((4, DEEP, 128), lambda i: (0, 0, 0)),
            pl.BlockSpec((4, DEEP, 128), lambda i: (15, 0, 0)),
            vmem(),
            vmem(),
        ],
        out_specs=(vmem(), vmem()),
        compiler_params=params(),
        name="assemble",
    )(info, state, state, from_west, from_east)


def exchange(state, to_east, to_west, info, turn):
    n_lat = lax.axis_size("lat")
    n_lon = lax.axis_size("lon")
    from_west = lax.ppermute(to_east, "lon", [(i, (i + 1) % n_lon) for i in range(n_lon)])
    from_east = lax.ppermute(to_west, "lon", [((i + 1) % n_lon, i) for i in range(n_lon)])
    one, two = assemble_call(info, state, from_west, from_east)
    got_one = lax.ppermute(one, ("lat", "lon"), perm_of(n_lat, n_lon, lambda a, b: (a ^ 1, b)))

    def branch(q):
        def rule(a, b):
            if a == n_lat - 1:
                return (a, q - b)
            if a == 0:
                return None
            return (((a + 1) ^ 1) - 1, b)

        return lambda v: lax.ppermute(v, ("lat", "lon"), perm_of(n_lat, n_lon, rule))

    got_two = lax.switch(turn, [branch(q) for q in range(n_lon)], two)
    return from_west, from_east, got_one, got_two


def diffuse_call(info, state, from_west, from_east, one, two, es):
    levels, ny, nx = es.shape
    out = pl.pallas_call(
        diffuse,
        out_shape=jax.ShapeDtypeStruct((levels * ny, nx), F32),
        in_specs=[smem()] + [vmem()] * 6,
        out_specs=vmem(),
        scratch_shapes=[
            pltpu.VMEM((ny + 8, DEEP, 2 * nx), F32),
            pltpu.VMEM((ny + 8, DEEP, 2 * nx), F32),
            pltpu.VMEM((5, ny + 8, 2 * nx), F32),
        ],
        compiler_params=params(),
        name="diffuse",
    )(info, state, from_west, from_east, one, two, es.reshape(levels * ny, nx))
    return out.reshape(levels, ny, nx)


def shards(
    background,
    error_scale,
    east_rate,
    north_rate,
    sea_mask,
    partner,
    obs_weight,
    obs_value,
    obs_error,
    obs_column,
    obs_count,
):
    levels = background.shape[0] * background.shape[1]
    ny = background.shape[2]
    nx = background.shape[3]
    capacity = obs_weight.shape[3]
    owners = obs_weight.shape[1]
    n_lat = lax.axis_size("lat")
    n_lon = lax.axis_size("lon")
    lat_at = lax.axis_index("lat").astype(jnp.int32)

    packed = pack_call(
        obs_count, jnp.swapaxes(obs_weight[0], 0, 1), obs_value[0], obs_error[0], obs_column[0]
    )
    received = lax.all_to_all(packed, ("lat", "lon"), split_axis=0, concat_axis=0, tiled=True)

    moved = (partner[0] - 3) % (nx * n_lon)
    turn = moved // nx
    info = jnp.stack([moved % nx, 1 - lat_at % 2, (lat_at == n_lat - 1).astype(jnp.int32), turn]).astype(jnp.int32)
    bg = background.reshape(levels, ny, nx)
    es = error_scale.reshape(levels, ny, nx)
    bgm = pl.pallas_call(
        split_background,
        out_shape=jax.ShapeDtypeStruct((64 * levels, 256), BF16),
        in_specs=[vmem()],
        out_specs=vmem(),
        compiler_params=params(),
        cost_estimate=pl.CostEstimate(flops=3000000, bytes_accessed=3300000, transcendentals=0),
        name="split_background",
    )(bg)

    state, to_east, to_west, cost = observe_call(received, bgm, east_rate, north_rate, sea_mask, es)
    state = state.reshape(ny, DEEP, nx)

    share = jnp.sum(cost)
    for axis, n in (("lon", n_lon), ("lat", n_lat)):
        shares = lax.all_to_all(jnp.broadcast_to(share, (n, 1, 128)), axis, split_axis=0, concat_axis=0, tiled=True)
        share = jnp.sum(shares[:, 0, 0])
    cost_share = share / (owners * owners * capacity)

    from_west, from_east, one, two = exchange(state, to_east, to_west, info, turn)
    increment = diffuse_call(info, state, from_west, from_east, one, two, es)
    return (increment.reshape(background.shape), cost_share)


def solution(mesh):
    in_specs = (
        P(None, None, "lat", "lon"),
        P(None, None, "lat", "lon"),
        P("lat", "lon"),
        P("lat", "lon"),
        P("lat", "lon"),
        P(),
        P(("lat", "lon"), None, None, None),
        P(("lat", "lon"), None, None),
        P(("lat", "lon"), None, None),
        P(("lat", "lon"), None, None),
        P(("lat", "lon"), None),
    )
    out_specs = (P(None, None, "lat", "lon"), P())
    return jax.shard_map(shards, mesh=mesh, in_specs=in_specs, out_specs=out_specs, check_vma=False)
```

time: 238 us -> 186 us (0.78); the launches traced: 237 us -> 182 us
  Pallas kernels: 125 us -> 80.1 us
  blocking collectives: 18.3 us -> 0 us
  waiting for transfers between devices: 50.7 us -> 55.7 us
  starting transfers between devices: 32 us -> 34.8 us
    pallas_call x6 -> x3, Pallas kernels: 112 us -> 67.9 us  [the longest x1 45.8 us: observe_call(): pl.pallas_call(observe, out_shape=(jax.ShapeDtypeStruct((ny * DEEP, nx),...]
    all_to_all x1, waiting for transfers between devices: 0.01 us -> 42.3 us  [shards(): lax.all_to_all(packed, ('lat', 'lon'), split_axis=0, concat_axis=0, tiled...]
    ppermute x2 -> x1, waiting for transfers between devices: 38.6 us -> 0.01 us  [exchange(): lax.ppermute(to_east, 'lon', [(i, (i + 1) % n_lon) for i in range(n_lon)])]
    all_to_all x1 -> x0, blocking collectives: 18.3 us -> none  [shards(): lax.all_to_all(jnp.broadcast_to(share, (owners, 1, 128)), ('lat', 'lon'),...]
    all_to_all x0 -> x2, starting transfers between devices: none -> 7.96 us  [shards(): lax.all_to_all(jnp.broadcast_to(share, (n, 1, 128)), axis, split_axis=0,...]
    all_to_all x0 -> x2, waiting for transfers between devices: none -> 7.3 us  [shards(): lax.all_to_all(jnp.broadcast_to(share, (n, 1, 128)), axis, split_axis=0,...]
    ppermute x2 -> x1, waiting for transfers between devices: 12.1 us -> 6.16 us  [branch(): lax.ppermute(v, ('lat', 'lon'), perm_of(n_lat, n_lon, rule))]
    ppermute x2 -> x1, starting transfers between devices: 8.83 us -> 3.97 us  [branch(): lax.ppermute(v, ('lat', 'lon'), perm_of(n_lat, n_lon, rule))]
  transfers between devices with their start and end apart: 9 -> 7, of which waited for: 4 -> 4; matrix products, arithmetic and copies ran while one was open for 2% -> 4% of each run, Pallas kernels for 3% -> 3%
where the time goes in v3:
time: 186 us; the launch traced here: 182 us
  Pallas kernels  80.1 us (43%)
  waiting for transfers between devices  55.7 us (30%)
  starting transfers between devices  34.8 us (19%)
  local copies, waits for them, and re-layouts  5.08 us (3%)
  other arithmetic  3.25 us (2%)
  between operations  3.16 us (2%)
    pallas_call x1, Pallas kernels, observe_call(): pl.pallas_call(observe, out_shape=(jax.ShapeDtypeStruct((ny * DEEP, nx),...  45.8 us
    all_to_all x1, waiting for transfers between devices, shards(): lax.all_to_all(packed, ('lat', 'lon'), split_axis=0, concat_axis=0, tiled...  42.3 us
    pallas_call x1, Pallas kernels, diffuse_call(): pl.pallas_call(diffuse, out_shape=jax.ShapeDtypeStruct((levels * ny, nx),...  19.1 us
    ppermute x1, starting transfers between devices, exchange(): lax.ppermute(to_west, 'lon', [((i + 1) % n_lon, i) for i in range(n_lon)])  12 us
    all_to_all x1, starting transfers between devices, shards(): lax.all_to_all(packed, ('lat', 'lon'), split_axis=0, concat_axis=0, tiled...  10.9 us
    pallas_call x1, Pallas kernels, pack_call(): pl.pallas_call(pack, grid=(owners // some,), out_shape=jax.ShapeDtypeStru...  9.13 us
    all_to_all x2, starting transfers between devices, shards(): lax.all_to_all(jnp.broadcast_to(share, (n, 1, 128)), axis, split_axis=0,...  7.96 us
    all_to_all x2, waiting for transfers between devices, shards(): lax.all_to_all(jnp.broadcast_to(share, (n, 1, 128)), axis, split_axis=0,...  7.3 us
  transfers between devices with their start and end apart: 7, of which 4 were waited for; matrix products, arithmetic and copies ran while one was open for 4% of the time, Pallas kernels for 3%

profile of v3, /device:TPU:6, one launch (start us, length us, event | category | flops | bytes accessed | tf_op | source)
XLA Modules:
  0.0 182.2 jit_solution(5446071204420811265)
XLA Ops:
  0.6 9.1 %pack.1 = f32[7168,128]{1,0:T(8,128)} custom-call(s32[1,128]{1,0:T(1,128)} %count_ref.1, f32[50,128,128]{2,1,0:T(8,128)} %bitcast.24, f32[128,128]{1,0:T(8,128)} %bitcast.27, f32[128,128]{1,0:T(8,128)} %bitcast.28, s32[128,128]{1,0:T(8,128)} %bitcast.29), custom_call_target="tpu_custom_call" | custom-call | tf_op jit(solution)/shard_map/pack/pallas_call | solution.py:90
  9.8 10.9 %all-to-all-start = ((f32[128,56,128]{2,1,0:T(8,128)}), f32[128,56,128]{2,1,0:T(8,128)}, u32[]{:S(2)}, u32[]{:S(2)}) async-start(f32[128,56,128]{2,1,0:T(8,128)} %bitcast.21), calls=%async_computation | async-start | bytes 7340032 | tf_op jit(solution)/shard_map/all_to_all | solution.py:498
  20.6 3.1 %split_background.1.bgm_ref = bf16[3200,256]{1,0:T(8,128)(2,1)} custom-call(f32[50,64,128]{2,1,0:T(8,128)} %bitcast.25), custom_call_target="tpu_custom_call" | custom-call | flops 3000000 | bytes 3300000 | tf_op jit(solution)/shard_map/split_background/pallas_call | solution.py:505
  23.7 42.3 %all-to-all-done = f32[128,56,128]{2,1,0:T(8,128)} async-done(((f32[128,56,128]{2,1,0:T(8,128)}), f32[128,56,128]{2,1,0:T(8,128)}, u32[]{:S(2)}, u32[]{:S(2)}) %all-to-all-start) | async-done | bytes 3670048 | tf_op jit(solution)/shard_map/all_to_all | solution.py:498
  66.0 45.8 %observe.1 = (f32[3584,128]{1,0:T(8,128)}, f32[56,768]{1,0:T(8,128)}, f32[56,384]{1,0:T(8,128)}, f32[1,2048]{1,0:T(1,128)}) custom-call(f32[7168,128]{1,0:T(8,128)} %bitcast.11.rec_ref, bf16[3200,256]{1,0:T(8,128)(2,1)} %split_background.1.bgm_ref, f32[64,128]{1,0:T(8,128)} %east_ref.1, f32[64,128]{1,0:T(8,128)} %north_ref.1, s32[64,128]{1,0:T(8,128)} %sea_ref.1, ...), custom_call_target="tpu_custom_call" | custom-call | tf_op jit(solution)/shard_map/observe/pallas_call | solution.py:255
  111.8 1.2 slice.9
  113.7 12.0 %collective-permute-start.17 = (f32[56,384]{1,0:T(8,128)}, f32[56,384]{1,0:T(8,128)S(1)}, u32[]{:S(2)}, u32[]{:S(2)}) collective-permute-start(f32[56,384]{1,0:T(8,128)} %get-tuple-element.43), channel_id=1, source_target_pairs={{1,0},{2,1},{3,2},{4,3},{5,4},{6,5},{7,6},{8,7},{9,8},{10,9},{11,1... | collective-permute-start | bytes 258056 | tf_op jit(solution)/shard_map/ppermute | solution.py:437
  125.7 1.4 reduce_sum.27
  127.1 1.3 broadcast_in_dim.6
  128.3 3.4 %all-to-all-start.1 = ((f32[16,1,128]{2,1,0:T(1,128)}), f32[16,1,128]{2,1,0:T(1,128)S(1)}, u32[]{:S(2)}, u32[]{:S(2)}) async-start(f32[16,1,128]{2,1,0:T(1,128)} %broadcast_in_dim.6), calls=%async_computation.1 | async-start | bytes 16384 | tf_op jit(solution)/shard_map/all_to_all | solution.py:520
  131.8 0.6 pad_add_fusion.info_ref
  132.4 0.6 copy-done.1
  133.1 3.0 %assemble.1 = (f32[4,56,256]{2,1,0:T(8,128)}, f32[4,56,256]{2,1,0:T(8,128)S(1)}) custom-call(s32[4]{0:T(128)} %pad_add_fusion.info_ref, f32[64,56,128]{2,1,0:T(8,128)} %bitcast.18, f32[64,56,128]{2,1,0:T(8,128)} %bitcast.19, f32[56,768]{1,0:T(8,128)} %copy-done, f32[56,384]{1,0:T(8,128)} %copy-done.1), custom_call_target="tpu_custom_call" | custom-call | tf_op jit(solution)/shard_map/assemble/pallas_call | solution.py:416
  136.1 3.2 %all-to-all-done.1 = f32[16,1,128]{2,1,0:T(1,128)S(1)} async-done(((f32[16,1,128]{2,1,0:T(1,128)}), f32[16,1,128]{2,1,0:T(1,128)S(1)}, u32[]{:S(2)}, u32[]{:S(2)}) %all-to-all-start.1) | async-done | bytes 8224 | tf_op jit(solution)/shard_map/all_to_all | solution.py:520
  139.3 0.7 slice_reduce_fusion
  140.0 1.2 broadcast_in_dim.7
  141.2 4.5 %all-to-all-start.2 = ((f32[8,1,128]{2,1,0:T(1,128)}), f32[8,1,128]{2,1,0:T(1,128)S(1)}, u32[]{:S(2)}, u32[]{:S(2)}) async-start(f32[8,1,128]{2,1,0:T(1,128)} %broadcast_in_dim.7), calls=%async_computation.2 | async-start | bytes 8192 | tf_op jit(solution)/shard_map/all_to_all | solution.py:520
  145.7 4.1 %all-to-all-done.2 = f32[8,1,128]{2,1,0:T(1,128)S(1)} async-done(((f32[8,1,128]{2,1,0:T(1,128)}), f32[8,1,128]{2,1,0:T(1,128)S(1)}, u32[]{:S(2)}, u32[]{:S(2)}) %all-to-all-start.2) | async-done | bytes 4128 | tf_op jit(solution)/shard_map/all_to_all | solution.py:520
  149.8 0.6 slice_reduce_fusion.1
  151.1 10.2 %conditional.1 = (f32[4,56,256]{2,1,0:T(8,128)}) conditional(s32[]{:T(128)} %clamp.3, f32[4,56,256]{2,1,0:T(8,128)S(1)} %get-tuple-element.45, f32[4,56,256]{2,1,0:T(8,128)S(1)} %get-tuple-element.45, f32[4,56,256]{2,1,0:T(8,128)S(1)} %get-tuple-element.45, f32[4,56,256]{2,1,0:T(8,128)S(1)} %get-tuple-element.45, ...), branch_computations={%region_0.1_spmd, %region_1.2_spmd, %region_2.3_spmd, %region_3.4_... | conditional | bytes 917552 | solution.py:451
  151.1 4.0 %collective-permute-start.3 = (f32[4,56,256]{2,1,0:T(8,128)S(1)}, f32[4,56,256]{2,1,0:T(8,128)}, u32[]{:S(2)}, u32[]{:S(2)}) collective-permute-start(f32[4,56,256]{2,1,0:T(8,128)S(1)} %param.3), channel_id=1, source_target_pairs={{16,32},{17,33},{18,34},{19,35},{20,36},{21,37},{22,38},{23,39},{2... | collective-permute-start | bytes 688136 | tf_op jit(solution)/shard_map/cond/branch_3_fun/ppermute | solution.py:449
  155.1 6.2 %collective-permute-done.3 = f32[4,56,256]{2,1,0:T(8,128)} collective-permute-done((f32[4,56,256]{2,1,0:T(8,128)S(1)}, f32[4,56,256]{2,1,0:T(8,128)}, u32[]{:S(2)}, u32[]{:S(2)}) %collective-permute-start.3) | collective-permute-done | bytes 229408 | tf_op jit(solution)/shard_map/cond/branch_3_fun/ppermute | solution.py:449
  161.2 0.7 copy-done.2
  161.9 19.1 %diffuse.1 = f32[3200,128]{1,0:T(8,128)} custom-call(s32[4]{0:T(128)} %pad_add_fusion.info_ref, f32[64,56,128]{2,1,0:T(8,128)} %bitcast.20, f32[56,768]{1,0:T(8,128)} %copy-done, f32[56,384]{1,0:T(8,128)} %copy-done.1, f32[4,56,256]{2,1,0:T(8,128)} %copy-done.2, f32[4,56,256]{2,1,0:T(8,128)} %get-tuple-element.47.two_ref, f32[3200,128]{1,0:T(8,128)} %bitcast.23), custom_call_target="tpu_custom_call" | custom-call | tf_op jit(solution)/shard_map/diffuse/pallas_call | solution.py:457
  (9 shorter events, 0.1 us)
Async XLA Ops:
  9.8 56.2 %all-to-all-start = ((f32[128,56,128]{2,1,0:T(8,128)}), f32[128,56,128]{2,1,0:T(8,128)}, u32[]{:S(2)}, u32[]{:S(2)}) async-start(f32[128,56,128]{2,1,0:T(8,128)} %bitcast.21), calls=%async_computation | async-start | bytes 7340032 | tf_op jit(solution)/shard_map/all_to_all | solution.py:498
  111.8 20.6 %collective-permute-start.16 = (f32[56,768]{1,0:T(8,128)}, f32[56,768]{1,0:T(8,128)S(1)}, u32[]{:S(2)}, u32[]{:S(2)}) collective-permute-start(f32[56,768]{1,0:T(8,128)} %get-tuple-element.42), channel_id=1, source_target_pairs={{0,1},{1,2},{2,3},{3,4},{4,5},{5,6},{6,7},{7,8},{8,9},{9,10},{10,1... | collective-permute-start | bytes 516104 | tf_op jit(solution)/shard_map/ppermute | solution.py:436
  113.7 18.7 %collective-permute-start.17 = (f32[56,384]{1,0:T(8,128)}, f32[56,384]{1,0:T(8,128)S(1)}, u32[]{:S(2)}, u32[]{:S(2)}) collective-permute-start(f32[56,384]{1,0:T(8,128)} %get-tuple-element.43), channel_id=1, source_target_pairs={{1,0},{2,1},{3,2},{4,3},{5,4},{6,5},{7,6},{8,7},{9,8},{10,9},{11,1... | collective-permute-start | bytes 258056 | tf_op jit(solution)/shard_map/ppermute | solution.py:437
  128.3 11.0 %all-to-all-start.1 = ((f32[16,1,128]{2,1,0:T(1,128)}), f32[16,1,128]{2,1,0:T(1,128)S(1)}, u32[]{:S(2)}, u32[]{:S(2)}) async-start(f32[16,1,128]{2,1,0:T(1,128)} %broadcast_in_dim.6), calls=%async_computation.1 | async-start | bytes 16384 | tf_op jit(solution)/shard_map/all_to_all | solution.py:520
  132.4 0.6 copy-start.1
  132.4 0.7 copy-start
  136.1 25.1 %collective-permute-start.18 = (f32[4,56,256]{2,1,0:T(8,128)}, f32[4,56,256]{2,1,0:T(8,128)S(1)}, u32[]{:S(2)}, u32[]{:S(2)}) collective-permute-start(f32[4,56,256]{2,1,0:T(8,128)} %get-tuple-element.44), channel_id=1, source_target_pairs={{0,16},{1,17},{2,18},{3,19},{4,20},{5,21},{6,22},{7,23},{8,24},{9,... | collective-permute-start | bytes 688136 | tf_op jit(solution)/shard_map/ppermute | solution.py:439
  141.2 8.6 %all-to-all-start.2 = ((f32[8,1,128]{2,1,0:T(1,128)}), f32[8,1,128]{2,1,0:T(1,128)S(1)}, u32[]{:S(2)}, u32[]{:S(2)}) async-start(f32[8,1,128]{2,1,0:T(1,128)} %broadcast_in_dim.7), calls=%async_computation.2 | async-start | bytes 8192 | tf_op jit(solution)/shard_map/all_to_all | solution.py:520
  151.1 10.1 %collective-permute-start.3 = (f32[4,56,256]{2,1,0:T(8,128)S(1)}, f32[4,56,256]{2,1,0:T(8,128)}, u32[]{:S(2)}, u32[]{:S(2)}) collective-permute-start(f32[4,56,256]{2,1,0:T(8,128)S(1)} %param.3), channel_id=1, source_target_pairs={{16,32},{17,33},{18,34},{19,35},{20,36},{21,37},{22,38},{23,39},{2... | collective-permute-start | bytes 688136 | tf_op jit(solution)/shard_map/cond/branch_3_fun/ppermute | solution.py:449
  161.2 0.7 copy-start.2

commit v4 on v3

--- a/solution.py
+++ b/solution.py
@@ -12,32 +12,24 @@
 BF16 = jnp.bfloat16
 WIDE = 2048
 DEEP = 56
-UNROLL_DIFFUSE = 4
+UNROLL_DIFFUSE = 7
 VMEM_LIMIT = 56 * 1024 * 1024
 
 
-def split_background(bg_ref, out_ref):
-    levels = bg_ref.shape[0]
-    for h in range(4):
-        for p in range(2):
-            base = (2 * h + p) * levels * 8
-            row = 32 * p + 8 * h
-
-            def body(i, _):
-                a = bg_ref[2 * i, row : row + 8, :]
-                b = bg_ref[2 * i + 1, row : row + 8, :]
-                x = jnp.concatenate([a, b], axis=0)
-                hi = x.astype(BF16)
-                lo = (x - hi.astype(F32)).astype(BF16)
-                at = pl.ds(pl.multiple_of(base + i * 16, 16), 16)
-                out_ref[at, 0:128] = hi
-                out_ref[at, 128:256] = lo
-                return 0
-
-            lax.fori_loop(0, levels // 2, body, 0, unroll=5)
-
-
-def pack(count_ref, w_ref, value_ref, error_ref, cell_ref, out_ref, order_ref, counts_ref):
+def pack(
+    partner_ref,
+    count_ref,
+    w_ref,
+    value_ref,
+    error_ref,
+    cell_ref,
+    bg_ref,
+    out_ref,
+    bgm_ref,
+    info_ref,
+    order_ref,
+    counts_ref,
+):
     levels, some, n = w_ref.shape
     owners = order_ref.shape[0]
     lane8 = lax.broadcasted_iota(jnp.int32, (8, n), 1)
@@ -66,6 +58,22 @@
             size *= 2
         order_ref[...] = x.astype(jnp.int32) & (n - 1)
 
+    span = n * lax.axis_size("lon")
+    moved = (partner_ref[0] + (span - 3)) % span
+    lat_at = lax.axis_index("lat")
+    info_ref[0] = moved % n
+    info_ref[1] = 1 - lat_at % 2
+    info_ref[2] = (lat_at == lax.axis_size("lat") - 1).astype(jnp.int32)
+    info_ref[3] = moved // n
+
+    for p in range(2):
+        for k in range(0, levels, 2):
+            x = jnp.concatenate([bg_ref[k, p, 0], bg_ref[k + 1, p, 0]], axis=0)
+            hi = x.astype(BF16)
+            at = p * 8 * levels + 8 * k
+            bgm_ref[at : at + 16, 0:128] = hi
+            bgm_ref[at : at + 16, 128:256] = (x - hi.astype(F32)).astype(BF16)
+
     for o in range(0, some, 8):
         at = pl.ds(pl.multiple_of(pl.program_id(0) * some + o, 8), 8)
         order = order_ref[at, :]
@@ -84,28 +92,41 @@
             put(k, jnp.zeros((8, n), F32))
 
 
-def pack_call(count, weight, value, error, column):
+def pack_call(partner, count, weight, value, error, column, bg):
     levels, owners, n = weight.shape
-    some = 16
+    ny, nx = bg.shape[1], bg.shape[2]
+    steps = 4
+    some = owners // steps
+    whole = lambda i: (0, 0)
     return pl.pallas_call(
         pack,
-        grid=(owners // some,),
-        out_shape=jax.ShapeDtypeStruct((owners * 56, n), F32),
+        grid=(steps,),
+        out_shape=(
+            jax.ShapeDtypeStruct((owners * DEEP, n), F32),
+            jax.ShapeDtypeStruct((levels * ny, 2 * nx), BF16),
+            jax.ShapeDtypeStruct((4,), jnp.int32),
+        ),
         in_specs=[
-            pl.BlockSpec((1, owners), lambda i: (0, 0)),
+            smem(),
+            pl.BlockSpec((1, owners), whole),
             pl.BlockSpec((levels, some, n), lambda i: (0, i, 0)),
-            pl.BlockSpec((owners, n), lambda i: (0, 0)),
-            pl.BlockSpec((owners, n), lambda i: (0, 0)),
-            pl.BlockSpec((owners, n), lambda i: (0, 0)),
+            pl.BlockSpec((owners, n), whole),
+            pl.BlockSpec((owners, n), whole),
+            pl.BlockSpec((owners, n), whole),
+            pl.BlockSpec((levels, 2, 1, 8, nx), lambda i: (0, 0, i, 0, 0)),
         ],
-        out_specs=pl.BlockSpec((some * 56, n), lambda i: (i, 0)),
+        out_specs=(
+            pl.BlockSpec((some * DEEP, n), lambda i: (i, 0)),
+            pl.BlockSpec((levels * ny // steps, 2 * nx), lambda i: (i, 0)),
+            smem(),
+        ),
         scratch_shapes=[pltpu.VMEM((owners, n), jnp.int32), pltpu.VMEM((owners, n), jnp.int32)],
         compiler_params=params(),
         name="pack",
-    )(count, weight, value, error, column)
-
-
-def observe(rec_ref, bgm_ref, east_ref, north_ref, sea_ref, es_ref, state_ref, to_east_ref, to_west_ref, cost_ref, tiles, force, whi, wlo, amat):
+    )(partner, count, weight, value, error, column, bg.reshape(levels, 2, 4, 8, nx))
+
+
+def observe(rec_ref, bgm_ref, east_ref, north_ref, sea_ref, es_ref, state_ref, to_east_ref, to_west_ref, total_ref, tiles, force, whi, wlo, amat, cost_ref):
     levels = es_ref.shape[0]
     sources = rec_ref.shape[0] // 56
     rows_in = 8 * levels
@@ -205,6 +226,8 @@
 
     lax.fori_loop(0, 8 * (total // wide), tile, 0)
 
+    total_ref[...] = jnp.broadcast_to(jnp.sum(cost_ref[...], axis=1, keepdims=True)[None], total_ref.shape)
+
     for r0 in range(0, 64, 8):
         b, part = (r0 // 8) % 4, r0 // 32
         sea = sea_ref[r0 : r0 + 8, :].astype(F32)
@@ -258,7 +281,7 @@
             jax.ShapeDtypeStruct((ny * DEEP, nx), F32),
             jax.ShapeDtypeStruct((DEEP, 768), F32),
             jax.ShapeDtypeStruct((DEEP, 384), F32),
-            jax.ShapeDtypeStruct((1, wide), F32),
+            jax.ShapeDtypeStruct((owners, 1, 128), F32),
         ),
         in_specs=[vmem()] * 6,
         out_specs=(vmem(),) * 4,
@@ -268,6 +291,7 @@
             pltpu.VMEM((56, wide), F32),
             pltpu.VMEM((56, wide), F32),
             pltpu.VMEM((8 * levels, 2 * wide), BF16),
+            pltpu.VMEM((1, wide), F32),
         ],
         compiler_params=params(),
         name="observe",
@@ -488,38 +512,19 @@
     nx = background.shape[3]
     capacity = obs_weight.shape[3]
     owners = obs_weight.shape[1]
-    n_lat = lax.axis_size("lat")
-    n_lon = lax.axis_size("lon")
-    lat_at = lax.axis_index("lat").astype(jnp.int32)
-
-    packed = pack_call(
-        obs_count, jnp.swapaxes(obs_weight[0], 0, 1), obs_value[0], obs_error[0], obs_column[0]
-    )
-    received = lax.all_to_all(packed, ("lat", "lon"), split_axis=0, concat_axis=0, tiled=True)
-
-    moved = (partner[0] - 3) % (nx * n_lon)
-    turn = moved // nx
-    info = jnp.stack([moved % nx, 1 - lat_at % 2, (lat_at == n_lat - 1).astype(jnp.int32), turn]).astype(jnp.int32)
     bg = background.reshape(levels, ny, nx)
     es = error_scale.reshape(levels, ny, nx)
-    bgm = pl.pallas_call(
-        split_background,
-        out_shape=jax.ShapeDtypeStruct((64 * levels, 256), BF16),
-        in_specs=[vmem()],
-        out_specs=vmem(),
-        compiler_params=params(),
-        cost_estimate=pl.CostEstimate(flops=3000000, bytes_accessed=3300000, transcendentals=0),
-        name="split_background",
-    )(bg)
-
+    packed, bgm, info = pack_call(
+        partner, obs_count, jnp.swapaxes(obs_weight[0], 0, 1), obs_value[0], obs_error[0], obs_column[0], bg
+    )
+    turn = info[3]
+    packed, bgm, info, turn = lax.optimization_barrier((packed, bgm, info, turn))
+    received = lax.all_to_all(packed, ("lat", "lon"), split_axis=0, concat_axis=0, tiled=True)
     state, to_east, to_west, cost = observe_call(received, bgm, east_rate, north_rate, sea_mask, es)
     state = state.reshape(ny, DEEP, nx)
 
-    share = jnp.sum(cost)
-    for axis, n in (("lon", n_lon), ("lat", n_lat)):
-        shares = lax.all_to_all(jnp.broadcast_to(share, (n, 1, 128)), axis, split_axis=0, concat_axis=0, tiled=True)
-        share = jnp.sum(shares[:, 0, 0])
-    cost_share = share / (owners * owners * capacity)
+    shares = lax.all_to_all(cost, ("lat", "lon"), split_axis=0, concat_axis=0, tiled=True)
+    cost_share = jnp.sum(shares[:, 0, 0]) / (owners * owners * capacity)
 
     from_west, from_east, one, two = exchange(state, to_east, to_west, info, turn)
     increment = diffuse_call(info, state, from_west, from_east, one, two, es)

time: 186 us -> 180 us (0.968); the launches traced: 182 us -> 181 us
  blocking collectives: 0 us -> 56.2 us
  waiting for transfers between devices: 55.7 us -> 22.3 us
  starting transfers between devices: 34.8 us -> 21.5 us
  Pallas kernels: 80.1 us -> 74.1 us
  other arithmetic: 3.25 us -> 0.73 us
  local copies, waits for them, and re-layouts: 5.08 us -> 2.56 us
    all_to_all x0 -> x1, blocking collectives: none -> 56.2 us  [shards(): lax.all_to_all(packed, ('lat', 'lon'), split_axis=0, concat_axis=0, tiled...]
    all_to_all x3 -> x1, waiting for transfers between devices: 49.6 us -> 7.29 us  [shards(): lax.all_to_all(cost, ('lat', 'lon'), split_axis=0, concat_axis=0, tiled=T...]
    all_to_all x3 -> x1, starting transfers between devices: 18.8 us -> 11.6 us  [shards(): lax.all_to_all(cost, ('lat', 'lon'), split_axis=0, concat_axis=0, tiled=T...]
    ppermute x1, starting transfers between devices: 12 us -> 5.06 us  [exchange(): lax.ppermute(to_west, 'lon', [((i + 1) % n_lon, i) for i in range(n_lon)])]
    ppermute x1, waiting for transfers between devices: 6.16 us -> 11.6 us  [branch(): lax.ppermute(v, ('lat', 'lon'), perm_of(n_lat, n_lon, rule))]
    pallas_call x2 -> x1, Pallas kernels: 12.2 us -> 7.84 us  [pack_call(): pl.pallas_call(pack, grid=(steps,), out_shape=(jax.ShapeDtypeStruct((owne...]
    broadcast_in_dim x2 -> x0, local copies, waits for them, and re-layouts: 2.5 us -> none  [shards(): jnp.broadcast_to(share, (n, 1, 128))]
    ppermute x1, waiting for transfers between devices: 0.01 us -> 2.41 us  [exchange(): lax.ppermute(to_west, 'lon', [((i + 1) % n_lon, i) for i in range(n_lon)])]
  transfers between devices with their start and end apart: 7 -> 5, of which waited for: 4 -> 4; matrix products, arithmetic and copies ran while one was open for 4% -> 0% of each run, Pallas kernels for 3% -> 0%
where the time goes in v4:
time: 180 us; the launch traced here: 181 us
  Pallas kernels  74.1 us (41%)
  blocking collectives  56.2 us (31%)
  waiting for transfers between devices  22.3 us (12%)
  starting transfers between devices  21.5 us (12%)
  between operations  3.08 us (2%)
  local copies, waits for them, and re-layouts  2.56 us (1%)
    all_to_all x1, blocking collectives, shards(): lax.all_to_all(packed, ('lat', 'lon'), split_axis=0, concat_axis=0, tiled...  56.2 us
    pallas_call x1, Pallas kernels, observe_call(): pl.pallas_call(observe, out_shape=(jax.ShapeDtypeStruct((ny * DEEP, nx),...  45.8 us
    pallas_call x1, Pallas kernels, diffuse_call(): pl.pallas_call(diffuse, out_shape=jax.ShapeDtypeStruct((levels * ny, nx),...  17.4 us
    ppermute x1, waiting for transfers between devices, branch(): lax.ppermute(v, ('lat', 'lon'), perm_of(n_lat, n_lon, rule))  11.6 us
    all_to_all x1, starting transfers between devices, shards(): lax.all_to_all(cost, ('lat', 'lon'), split_axis=0, concat_axis=0, tiled=T...  11.6 us
    pallas_call x1, Pallas kernels, pack_call(): pl.pallas_call(pack, grid=(steps,), out_shape=(jax.ShapeDtypeStruct((owne...  7.84 us
    all_to_all x1, waiting for transfers between devices, shards(): lax.all_to_all(cost, ('lat', 'lon'), split_axis=0, concat_axis=0, tiled=T...  7.29 us
    ppermute x1, starting transfers between devices, exchange(): lax.ppermute(to_west, 'lon', [((i + 1) % n_lon, i) for i in range(n_lon)])  5.06 us
  transfers between devices with their start and end apart: 5, of which 4 were waited for; matrix products, arithmetic and copies ran while one was open for 0% of the time, Pallas kernels for 0%

profile of v4, /device:TPU:6, one launch (start us, length us, event | category | flops | bytes accessed | tf_op | source)
XLA Modules:
  0.0 180.6 jit_solution(11614999576586239684)
XLA Ops:
  0.6 7.8 %pack.1 = (f32[7168,128]{1,0:T(8,128)}, bf16[3200,256]{1,0:T(8,128)(2,1)}, s32[4]{0:T(128)}) custom-call(s32[2048]{0:T(1024)} %partner_ref.1, s32[1,128]{1,0:T(1,128)} %count_ref.1, f32[50,128,128]{2,1,0:T(8,128)} %bitcast.21, f32[128,128]{1,0:T(8,128)} %bitcast.24, f32[128,128]{1,0:T(8,128)} %bitcast.25, s32[128,128]{1,0:T(8,128)} %bitcast.26, ...), custom_call_target="tpu_custom_call" | custom-call | tf_op jit(solution)/shard_map/pack/pallas_call | solution.py:101
  8.5 1.2 slice.6
  9.7 56.2 %all_to_all.16 = f32[128,56,128]{2,1,0:T(8,128)} all-to-all(f32[128,56,128]{2,1,0:T(8,128)} %bitcast.20), channel_id=1, replica_groups=mesh['lat'=8,'lon'=16] {'lat','lon'}, dimensions={0} | all-to-all | bytes 7340032 | tf_op jit(solution)/shard_map/all_to_all | solution.py:522
  65.9 45.8 %observe.1 = (f32[3584,128]{1,0:T(8,128)}, f32[56,768]{1,0:T(8,128)}, f32[56,384]{1,0:T(8,128)}, f32[128,1,128]{2,1,0:T(1,128)}) custom-call(f32[7168,128]{1,0:T(8,128)} %bitcast.17, bf16[3200,256]{1,0:T(8,128)(2,1)} %get-tuple-element.53.bgm_ref, f32[64,128]{1,0:T(8,128)} %east_ref.1, f32[64,128]{1,0:T(8,128)} %north_ref.1, s32[64,128]{1,0:T(8,128)} %sea_ref.1, ...), custom_call_target="tpu_custom_call" | custom-call | tf_op jit(solution)/shard_map/observe/pallas_call | solution.py:278
  111.7 0.6 collective-permute-start.16
  112.3 5.1 %collective-permute-start.17 = (f32[56,384]{1,0:T(8,128)}, f32[56,384]{1,0:T(8,128)S(1)}, u32[]{:S(2)}, u32[]{:S(2)}) collective-permute-start(f32[56,384]{1,0:T(8,128)} %get-tuple-element.56), channel_id=1, source_target_pairs={{1,0},{2,1},{3,2},{4,3},{5,4},{6,5},{7,6},{8,7},{9,8},{10,9},{11,1... | collective-permute-start | bytes 258056 | tf_op jit(solution)/shard_map/ppermute | solution.py:461
  117.4 2.4 %collective-permute-done.17.fe_ref = f32[56,384]{1,0:T(8,128)S(1)} collective-permute-done((f32[56,384]{1,0:T(8,128)}, f32[56,384]{1,0:T(8,128)S(1)}, u32[]{:S(2)}, u32[]{:S(2)}) %collective-permute-start.17) | collective-permute-done | bytes 86048 | tf_op jit(solution)/shard_map/ppermute | solution.py:461
  119.8 0.0 copy-start.1
  119.8 0.9 collective-permute-done.16.fw_ref
  120.7 0.0 copy-start
  120.7 0.0 copy-done.1
  120.7 0.7 copy-done
  121.4 3.0 %assemble.1 = (f32[4,56,256]{2,1,0:T(8,128)}, f32[4,56,256]{2,1,0:T(8,128)S(1)}) custom-call(s32[4]{0:T(128)} %get-tuple-element.51.info_ref, f32[64,56,128]{2,1,0:T(8,128)} %bitcast.14, f32[64,56,128]{2,1,0:T(8,128)} %bitcast.15, f32[56,768]{1,0:T(8,128)} %copy-done, f32[56,384]{1,0:T(8,128)} %copy-done.1), custom_call_target="tpu_custom_call" | custom-call | tf_op jit(solution)/shard_map/assemble/pallas_call | solution.py:440
  124.4 0.0 collective-permute-start.18
  124.4 11.6 %all-to-all-start.1 = ((f32[128,1,128]{2,1,0:T(1,128)}), f32[128,1,128]{2,1,0:T(1,128)S(1)}, u32[]{:S(2)}, u32[]{:S(2)}) async-start(f32[128,1,128]{2,1,0:T(1,128)} %get-tuple-element.60), calls=%async_computation.1 | async-start | bytes 131072 | tf_op jit(solution)/shard_map/all_to_all | solution.py:526
  136.7 7.3 %all-to-all-done.1 = f32[128,1,128]{2,1,0:T(1,128)S(1)} async-done(((f32[128,1,128]{2,1,0:T(1,128)}), f32[128,1,128]{2,1,0:T(1,128)S(1)}, u32[]{:S(2)}, u32[]{:S(2)}) %all-to-all-start.1) | async-done | bytes 65568 | tf_op jit(solution)/shard_map/all_to_all | solution.py:526
  144.0 0.7 slice_reduce_fusion
  145.4 16.0 %conditional.1 = (f32[4,56,256]{2,1,0:T(8,128)}) conditional(s32[]{:T(128)} %clamp.3, f32[4,56,256]{2,1,0:T(8,128)S(1)} %get-tuple-element.59, f32[4,56,256]{2,1,0:T(8,128)S(1)} %get-tuple-element.59, f32[4,56,256]{2,1,0:T(8,128)S(1)} %get-tuple-element.59, f32[4,56,256]{2,1,0:T(8,128)S(1)} %get-tuple-element.59, ...), branch_computations={%region_0.0_spmd, %region_1.0_spmd, %region_2.0_spmd, %region_3.0_... | conditional | bytes 917552 | solution.py:475
  145.4 4.3 %collective-permute-start.15 = (f32[4,56,256]{2,1,0:T(8,128)S(1)}, f32[4,56,256]{2,1,0:T(8,128)}, u32[]{:S(2)}, u32[]{:S(2)}) collective-permute-start(f32[4,56,256]{2,1,0:T(8,128)S(1)} %param.15), channel_id=1, source_target_pairs={{16,32},{17,33},{18,34},{19,35},{20,36},{21,37},{22,38},{23,39},{2... | collective-permute-start | bytes 688136 | tf_op jit(solution)/shard_map/cond/branch_15_fun/ppermute | solution.py:473
  149.7 11.6 %collective-permute-done.15 = f32[4,56,256]{2,1,0:T(8,128)} collective-permute-done((f32[4,56,256]{2,1,0:T(8,128)S(1)}, f32[4,56,256]{2,1,0:T(8,128)}, u32[]{:S(2)}, u32[]{:S(2)}) %collective-permute-start.15) | collective-permute-done | bytes 229408 | tf_op jit(solution)/shard_map/cond/branch_15_fun/ppermute | solution.py:473
  161.3 0.0 collective-permute-done.18.one_ref
  161.3 0.0 copy-start.2
  161.3 0.7 copy-done.2
  162.0 17.4 %diffuse.1 = f32[3200,128]{1,0:T(8,128)} custom-call(s32[4]{0:T(128)} %get-tuple-element.51.info_ref, f32[64,56,128]{2,1,0:T(8,128)} %bitcast.16, f32[56,768]{1,0:T(8,128)} %copy-done, f32[56,384]{1,0:T(8,128)} %copy-done.1, f32[4,56,256]{2,1,0:T(8,128)} %copy-done.2, f32[4,56,256]{2,1,0:T(8,128)} %get-tuple-element.61.two_ref, f32[3200,128]{1,0:T(8,128)} %bitcast.19), custom_call_target="tpu_custom_call" | custom-call | tf_op jit(solution)/shard_map/diffuse/pallas_call | solution.py:481
Async XLA Ops:
  111.7 9.0 %collective-permute-start.16 = (f32[56,768]{1,0:T(8,128)}, f32[56,768]{1,0:T(8,128)S(1)}, u32[]{:S(2)}, u32[]{:S(2)}) collective-permute-start(f32[56,768]{1,0:T(8,128)} %get-tuple-element.55), channel_id=1, source_target_pairs={{0,1},{1,2},{2,3},{3,4},{4,5},{5,6},{6,7},{7,8},{8,9},{9,10},{10,1... | collective-permute-start | bytes 516104 | tf_op jit(solution)/shard_map/ppermute | solution.py:460
  112.3 7.5 %collective-permute-start.17 = (f32[56,384]{1,0:T(8,128)}, f32[56,384]{1,0:T(8,128)S(1)}, u32[]{:S(2)}, u32[]{:S(2)}) collective-permute-start(f32[56,384]{1,0:T(8,128)} %get-tuple-element.56), channel_id=1, source_target_pairs={{1,0},{2,1},{3,2},{4,3},{5,4},{6,5},{7,6},{8,7},{9,8},{10,9},{11,1... | collective-permute-start | bytes 258056 | tf_op jit(solution)/shard_map/ppermute | solution.py:461
  119.8 0.9 copy-start.1
  120.7 0.7 copy-start
  124.4 36.9 %collective-permute-start.18 = (f32[4,56,256]{2,1,0:T(8,128)}, f32[4,56,256]{2,1,0:T(8,128)S(1)}, u32[]{:S(2)}, u32[]{:S(2)}) collective-permute-start(f32[4,56,256]{2,1,0:T(8,128)} %get-tuple-element.57), channel_id=1, source_target_pairs={{0,16},{1,17},{2,18},{3,19},{4,20},{5,21},{6,22},{7,23},{8,24},{9,... | collective-permute-start | bytes 688136 | tf_op jit(solution)/shard_map/ppermute | solution.py:463
  124.4 19.5 %all-to-all-start.1 = ((f32[128,1,128]{2,1,0:T(1,128)}), f32[128,1,128]{2,1,0:T(1,128)S(1)}, u32[]{:S(2)}, u32[]{:S(2)}) async-start(f32[128,1,128]{2,1,0:T(1,128)} %get-tuple-element.60), calls=%async_computation.1 | async-start | bytes 131072 | tf_op jit(solution)/shard_map/all_to_all | solution.py:526
  145.4 15.9 %collective-permute-start.15 = (f32[4,56,256]{2,1,0:T(8,128)S(1)}, f32[4,56,256]{2,1,0:T(8,128)}, u32[]{:S(2)}, u32[]{:S(2)}) collective-permute-start(f32[4,56,256]{2,1,0:T(8,128)S(1)} %param.15), channel_id=1, source_target_pairs={{16,32},{17,33},{18,34},{19,35},{20,36},{21,37},{22,38},{23,39},{2... | collective-permute-start | bytes 688136 | tf_op jit(solution)/shard_map/cond/branch_15_fun/ppermute | solution.py:473
  161.3 0.7 copy-start.2
